TPU v7x, 512 devices: a whole 4x4x16 slice. The times are simulated.
512 devices in a mesh: front: 16 (over y, x), tile: 32 (over z, core).
Axes of the slice: x: 4, y: 4, z: 16, core: 2. Of those that a mesh axis runs over, the one named last changes fastest.
Arguments:
- pool: bfloat16 [16, 32768, 256], P('front', 'tile'), may hold values from -6 to 6
- nbr_owner: int32 [16, 256, 1024, 1], P('front', 'tile'), may hold values from 0 to 31; in each aligned block of 8192 rows (0 to 8191, 8192 to 16383, ..., all dimensions but the last counted through in order) at most 512 rows name the same one
- nbr_row: int32 [16, 256, 1024], P('front', 'tile'), may hold values from 0 to 1023
- nbr_count: int32 [16, 256], P('front', 'tile'), may hold values from 512 to 1024
- normal_draw: bfloat16 [16, 256, 256, 256], P('front', 'tile'), may hold values from -6 to 6
- kriging_weight: bfloat16 [256, 1024], replicated, may hold values from -0.1875 to 0.1875
- noise_factor: bfloat16 [256, 256], replicated, may hold values from -0.375 to 0.375
- face_weight: float32 [256, 32], replicated, may hold values from -1 to 1
Outputs:
- evolved: bfloat16 [16, 256, 256, 256], P('front', 'tile')
Inputs may be any that keep to these rules, and one draw needn't show every extreme that they name: `nbr_owner`: among the entries of one device's blocks, no owner is named by more than 512 entries, a bound that some block reaches.
All inputs are finite; a program needn't handle non-finite values.
Results may differ from a plain program's by a relative error of at most 0.0013.
Values may be sent and summed in bfloat16 or wider, within the bound.
No kernel may reach another device: no remote copies, remote signals or barrier semaphores. Data moves between devices by JAX's collectives and lax.ppermute only.
A program may use at most 64 MiB of HBM per device.

v0:
```python
import jax
import jax.numpy as jnp
from jax import lax
from jax.sharding import PartitionSpec as P


def from_behind(value, axis, steps):
    count = lax.axis_size(axis)
    initial, last = (max(0, -steps), min(count, count - steps))
    return lax.ppermute(value, axis, [(source, source + steps) for source in range(initial, last)])


def body(
    pool, nbr_owner, nbr_row, nbr_count, normal_draw, kriging_weight, noise_factor, face_weight
):
    tile_count = lax.axis_size("tile")
    blocks = nbr_row.shape[1]
    neighbours = nbr_row.shape[2]
    realizations = pool.shape[2]
    block_cells = kriging_weight.shape[0]
    face_cells = face_weight.shape[1]
    owners = nbr_owner.reshape(-1)
    pool_index = nbr_row.reshape(-1)
    local_pool = pool[0]
    capacity = 2 * blocks * neighbours // tile_count
    onehot = (jnp.arange(tile_count, dtype=jnp.int32)[:, None] == owners[None, :]).astype(jnp.int32)
    earlier_count = jnp.cumsum(onehot, axis=1) - onehot
    slot_of = jnp.sum(earlier_count * onehot, axis=0)
    requests = jnp.zeros((tile_count, capacity), jnp.int32).at[owners, slot_of].set(pool_index)
    found_rows = jnp.take(
        local_pool,
        lax.all_to_all(requests, "tile", split_axis=0, concat_axis=0, tiled=True),
        axis=0,
    )
    answers = lax.all_to_all(found_rows, "tile", split_axis=0, concat_axis=0, tiled=True)
    values = answers[owners, slot_of]
    values = values.reshape(blocks, neighbours, realizations)
    is_live = jnp.arange(neighbours)[None, :] < nbr_count[0][:, None]
    values = jnp.where(is_live[:, :, None], values, jnp.zeros((), values.dtype))
    lower_factor = jnp.tril(noise_factor)
    local_part = jnp.einsum(
        "cn,bnr->bcr", kriging_weight, values, preferred_element_type=jnp.float32
    )
    local_part = local_part + jnp.einsum(
        "cd,bdr->bcr", lower_factor, normal_draw[0], preferred_element_type=jnp.float32
    )
    local_face = local_part[:, block_cells - face_cells :, :]
    face_square = face_weight[block_cells - face_cells :, :]
    front_index = lax.axis_index("front")
    front_count = lax.axis_size("front")

    def section(section_no, carry):
        own_edge, received = carry
        incoming = from_behind(own_edge, "front", 1)
        updated = local_face + jnp.einsum(
            "ce,ber->bcr", face_square, incoming, precision=lax.Precision.HIGHEST
        )
        is_mine = front_index == section_no
        return (jnp.where(is_mine, updated, own_edge), jnp.where(is_mine, incoming, received))

    empty_edge = jnp.zeros_like(local_face)
    own_edge, received = lax.fori_loop(0, front_count, section, (empty_edge, empty_edge))
    state = local_part + jnp.einsum(
        "ce,ber->bcr", face_weight, received, precision=lax.Precision.HIGHEST
    )
    return state.astype(jnp.bfloat16)[None]


def solution(mesh):
    placed = (
        P("front", "tile", None),
        P("front", "tile", None, None),
        P("front", "tile", None),
        P("front", "tile"),
        P("front", "tile", None, None),
        P(),
        P(),
        P(),
    )
    return jax.shard_map(
        body, mesh=mesh, in_specs=placed, out_specs=P("front", "tile", None, None), check_vma=False
    )
```

profile of v0, /device:TPU:48, one launch (start us, length us, event | category | flops | bytes accessed | tf_op | source)
XLA Modules:
  0.0 862.2 jit_solution(2146487166756964524)
XLA Ops:
  0.0 2.0 fusion.10
  2.0 17.1 %reduce-window.6 = s32[32,64,128]{2,1,0:T(8,128)S(1)} reduce-window(s32[32,64,128]{2,1,0:T(8,128)} %fusion.10, s32[]{:T(128)} %constant.39.clone.1), window={size=1x1x128 pad=0_0x0_0x127_0}, to_apply=%region_0.0 | reduce-window | flops 33292288 | bytes 2097156 | tf_op jit(solution)/shard_map/reduce-window
  21.2 30.5 %scatter_custom_fusion = s32[16384]{0:T(1024)S(1)} fusion(s32[8192]{0:T(1024)S(1)} %broadcast_select_fusion.2, s32[8192]{0:T(1024)S(1)} %bitcast.74, s32[]{:T(128)} %constant.39.clone.1), kind=kCustom, calls=%fused_computation.40 | custom fusion | bytes 65540
  51.7 28.3 %all_to_all.20 = s32[32,1,512]{2,1,0:T(1,128)S(1)} all-to-all(s32[32,1,512]{2,1,0:T(1,128)S(1)} %bitcast.69), channel_id=1, replica_groups=mesh['front'=16,'tile'=32] {'tile'}, dimensions={0} | all-to-all | bytes 131072 | tf_op jit(solution)/shard_map/all_to_all | solution.py:32
  80.1 64.8 %gather_fusion = bf16[16384,256]{1,0:T(8,128)(2,1)} fusion(bf16[1024,256]{1,0:T(8,128)(2,1)S(1)} %bitcast.62, s32[16384]{0:T(1024)S(1)} %broadcast_clamp_fusion), kind=kCustom, calls=%fused_computation | custom fusion | bytes 16842752 | tf_op jit(solution)/shard_map/jit(_take)/gather | solution.py:30
  145.0 8.1 broadcast_select_fusion.1
  153.0 6.1 all-to-all-start.1
  159.4 369.8 %all-to-all-done.1 = bf16[32,512,256]{2,1,0:T(8,128)(2,1)} async-done(((bf16[32,512,256]{2,1,0:T(8,128)(2,1)}), bf16[32,512,256]{2,1,0:T(8,128)(2,1)}, u32[]{:S(2)}, u32[]{:S(2)}) %all-to-all-start.1) | async-done | bytes 8388640 | tf_op jit(solution)/shard_map/all_to_all | solution.py:35
  529.2 137.6 %gather_fusion.1 = bf16[8192,256]{1,0:T(8,128)(2,1)} fusion(bf16[32,512,256]{2,1,0:T(8,128)(2,1)} %all-to-all-done.1, s32[8192]{0:T(1024)S(1)} %bitcast.63), kind=kCustom, calls=%fused_computation.1 | custom fusion | bytes 8454144 | tf_op jit(solution)/shard_map/gather | solution.py:36
  666.9 4.3 fusion.3
  673.0 184.7 %while.16 = (s32[]{:T(128)}, f32[8,32,256]{2,1,0:T(8,128)S(1)}, f32[8,32,256]{2,1,0:T(8,128)S(1)}, s32[]{:T(128)}, f32[32,32]{1,0:T(8,128)S(1)}, /*index=5*/f32[8,32,256]{2,1,0:T(8,128)S(1)}, s32[]{:T(128)}, s32[]{:T(128)}) while((s32[]{:T(128)}, f32[8,32,256]{2,1,0:T(8,128)S(1)}, f32[8,32,256]{2,1,0:T(8,128)S(1)}, s32[]{:T(128)}, ...), condition=%wide.region_5.6_spmd.clone, body=%wide.region_4.5_spmd.clone.sunk | while | flops 25493508 | bytes 3412115 | solution.py:62
  673.1 3.6 collective-permute-start
  676.7 8.4 collective-permute-done
  687.6 9.3 %collective-permute-done = f32[8,32,256]{2,1,0:T(8,128)S(1)} collective-permute-done((f32[8,32,256]{2,1,0:T(8,128)S(1)}, f32[8,32,256]{2,1,0:T(8,128)S(1)}, u32[]{:S(2)}, u32[]{:S(2)}) %collective-permute-start) | collective-permute-done | bytes 262176 | tf_op jit(solution)/shard_map/while/body/eval_jaxpr/ppermute | solution.py:10
  699.3 8.4 collective-permute-done
  710.2 8.4 collective-permute-done
  719.1 1.9 collective-permute-start
  721.1 8.4 collective-permute-done
  730.0 1.9 collective-permute-start
  731.9 8.4 collective-permute-done
  740.9 1.9 collective-permute-start
  742.8 8.9 %collective-permute-done = f32[8,32,256]{2,1,0:T(8,128)S(1)} collective-permute-done((f32[8,32,256]{2,1,0:T(8,128)S(1)}, f32[8,32,256]{2,1,0:T(8,128)S(1)}, u32[]{:S(2)}, u32[]{:S(2)}) %collective-permute-start) | collective-permute-done | bytes 262176 | tf_op jit(solution)/shard_map/while/body/eval_jaxpr/ppermute | solution.py:10
  754.2 10.1 %collective-permute-done = f32[8,32,256]{2,1,0:T(8,128)S(1)} collective-permute-done((f32[8,32,256]{2,1,0:T(8,128)S(1)}, f32[8,32,256]{2,1,0:T(8,128)S(1)}, u32[]{:S(2)}, u32[]{:S(2)}) %collective-permute-start) | collective-permute-done | bytes 262176 | tf_op jit(solution)/shard_map/while/body/eval_jaxpr/ppermute | solution.py:10
  766.7 11.2 %collective-permute-done = f32[8,32,256]{2,1,0:T(8,128)S(1)} collective-permute-done((f32[8,32,256]{2,1,0:T(8,128)S(1)}, f32[8,32,256]{2,1,0:T(8,128)S(1)}, u32[]{:S(2)}, u32[]{:S(2)}) %collective-permute-start) | collective-permute-done | bytes 262176 | tf_op jit(solution)/shard_map/while/body/eval_jaxpr/ppermute | solution.py:10
  780.3 10.4 %collective-permute-done = f32[8,32,256]{2,1,0:T(8,128)S(1)} collective-permute-done((f32[8,32,256]{2,1,0:T(8,128)S(1)}, f32[8,32,256]{2,1,0:T(8,128)S(1)}, u32[]{:S(2)}, u32[]{:S(2)}) %collective-permute-start) | collective-permute-done | bytes 262176 | tf_op jit(solution)/shard_map/while/body/eval_jaxpr/ppermute | solution.py:10
  793.1 9.6 %collective-permute-done = f32[8,32,256]{2,1,0:T(8,128)S(1)} collective-permute-done((f32[8,32,256]{2,1,0:T(8,128)S(1)}, f32[8,32,256]{2,1,0:T(8,128)S(1)}, u32[]{:S(2)}, u32[]{:S(2)}) %collective-permute-start) | collective-permute-done | bytes 262176 | tf_op jit(solution)/shard_map/while/body/eval_jaxpr/ppermute | solution.py:10
  805.1 8.6 %collective-permute-done = f32[8,32,256]{2,1,0:T(8,128)S(1)} collective-permute-done((f32[8,32,256]{2,1,0:T(8,128)S(1)}, f32[8,32,256]{2,1,0:T(8,128)S(1)}, u32[]{:S(2)}, u32[]{:S(2)}) %collective-permute-start) | collective-permute-done | bytes 262176 | tf_op jit(solution)/shard_map/while/body/eval_jaxpr/ppermute | solution.py:10
  816.2 8.4 collective-permute-done
  827.0 8.4 collective-permute-done
  837.9 8.4 collective-permute-done
  848.8 8.4 collective-permute-done
  857.7 4.5 fusion.8
  (100 shorter events, 34.5 us)
Async XLA Ops:
  0.0 671.2 %copy-start = (bf16[1,8,256,256]{3,2,1,0:T(8,128)(2,1)S(1)}, bf16[1,8,256,256]{3,2,1,0:T(8,128)(2,1)}, u32[]{:S(2)}) copy-start(bf16[1,8,256,256]{3,2,1,0:T(8,128)(2,1)} %param.14) | copy-start | bytes 3145732
  0.0 20.8 %copy-start.8 = (s32[2]{0:T(128)S(1)}, s32[2]{0:T(128)}, u32[]{:S(2)}) copy-start(s32[2]{0:T(128)} %constant.54) | copy-start | bytes 28
  0.0 20.9 %copy-start.7 = (s32[2]{0:T(128)S(1)}, s32[2]{0:T(128)}, u32[]{:S(2)}) copy-start(s32[2]{0:T(128)} %constant.57) | copy-start | bytes 28
  0.0 20.3 %copy-start.3 = (s32[1,8,1024,1]{2,3,1,0:T(1,128)S(1)}, s32[1,8,1024,1]{2,3,1,0:T(1,128)}, u32[]{:S(2)}) copy-start(s32[1,8,1024,1]{2,3,1,0:T(1,128)} %param.11) | copy-start | bytes 98308
  0.0 21.1 %copy-start.6 = (s32[1,8,1024]{2,1,0:T(8,128)S(1)}, s32[1,8,1024]{2,1,0:T(8,128)}, u32[]{:S(2)}) copy-start(s32[1,8,1024]{2,1,0:T(8,128)} %param.12) | copy-start | bytes 98308
  0.0 80.1 %copy-start.1 = (bf16[1,1024,256]{2,1,0:T(8,128)(2,1)S(1)}, bf16[1,1024,256]{2,1,0:T(8,128)(2,1)}, u32[]{:S(2)}) copy-start(bf16[1,1024,256]{2,1,0:T(8,128)(2,1)} %param.10) | copy-start | bytes 1572868
  153.0 6.2 copy-start.5
  153.0 6.3 copy-start.9
  153.0 376.2 %all-to-all-start.1 = ((bf16[32,512,256]{2,1,0:T(8,128)(2,1)}), bf16[32,512,256]{2,1,0:T(8,128)(2,1)}, u32[]{:S(2)}, u32[]{:S(2)}) async-start(bf16[32,512,256]{2,1,0:T(8,128)(2,1)} %broadcast_select_fusion.1), calls=%async_computation.1 | async-start | bytes 16777216 | tf_op jit(solution)/shard_map/all_to_all | solution.py:35
  529.2 137.6 %copy-start.10 = (bf16[256,1024]{1,0:T(8,128)(2,1)S(1)}, bf16[256,1024]{1,0:T(8,128)(2,1)}, u32[]{:S(2)}) copy-start(bf16[256,1024]{1,0:T(8,128)(2,1)} %param.15) | copy-start | bytes 1572868
  666.9 4.3 copy-start.4
  671.6 1.4 copy-start.2
  673.1 12.1 %collective-permute-start = (f32[8,32,256]{2,1,0:T(8,128)S(1)}, f32[8,32,256]{2,1,0:T(8,128)S(1)}, u32[]{:S(2)}, u32[]{:S(2)}) collective-permute-start(f32[8,32,256]{2,1,0:T(8,128)S(1)} %broadcast_select_fusion.4), channel_id=1, source_target_pairs={{0,32},{32,64},{64,96},{96,128},{128,160},{160,192},{192,224},{224... | collective-permute-start | bytes 786440 | tf_op jit(solution)/shard_map/while/body/eval_jaxpr/ppermute | solution.py:10
  685.7 11.2 %collective-permute-start = (f32[8,32,256]{2,1,0:T(8,128)S(1)}, f32[8,32,256]{2,1,0:T(8,128)S(1)}, u32[]{:S(2)}, u32[]{:S(2)}) collective-permute-start(f32[8,32,256]{2,1,0:T(8,128)S(1)} %broadcast_select_fusion.4), channel_id=1, source_target_pairs={{0,32},{32,64},{64,96},{96,128},{128,160},{160,192},{192,224},{224... | collective-permute-start | bytes 786440 | tf_op jit(solution)/shard_map/while/body/eval_jaxpr/ppermute | solution.py:10
  697.4 10.4 %collective-permute-start = (f32[8,32,256]{2,1,0:T(8,128)S(1)}, f32[8,32,256]{2,1,0:T(8,128)S(1)}, u32[]{:S(2)}, u32[]{:S(2)}) collective-permute-start(f32[8,32,256]{2,1,0:T(8,128)S(1)} %broadcast_select_fusion.4), channel_id=1, source_target_pairs={{0,32},{32,64},{64,96},{96,128},{128,160},{160,192},{192,224},{224... | collective-permute-start | bytes 786440 | tf_op jit(solution)/shard_map/while/body/eval_jaxpr/ppermute | solution.py:10
  708.3 10.4 %collective-permute-start = (f32[8,32,256]{2,1,0:T(8,128)S(1)}, f32[8,32,256]{2,1,0:T(8,128)S(1)}, u32[]{:S(2)}, u32[]{:S(2)}) collective-permute-start(f32[8,32,256]{2,1,0:T(8,128)S(1)} %broadcast_select_fusion.4), channel_id=1, source_target_pairs={{0,32},{32,64},{64,96},{96,128},{128,160},{160,192},{192,224},{224... | collective-permute-start | bytes 786440 | tf_op jit(solution)/shard_map/while/body/eval_jaxpr/ppermute | solution.py:10
  719.1 10.4 %collective-permute-start = (f32[8,32,256]{2,1,0:T(8,128)S(1)}, f32[8,32,256]{2,1,0:T(8,128)S(1)}, u32[]{:S(2)}, u32[]{:S(2)}) collective-permute-start(f32[8,32,256]{2,1,0:T(8,128)S(1)} %broadcast_select_fusion.4), channel_id=1, source_target_pairs={{0,32},{32,64},{64,96},{96,128},{128,160},{160,192},{192,224},{224... | collective-permute-start | bytes 786440 | tf_op jit(solution)/shard_map/while/body/eval_jaxpr/ppermute | solution.py:10
  730.0 10.4 %collective-permute-start = (f32[8,32,256]{2,1,0:T(8,128)S(1)}, f32[8,32,256]{2,1,0:T(8,128)S(1)}, u32[]{:S(2)}, u32[]{:S(2)}) collective-permute-start(f32[8,32,256]{2,1,0:T(8,128)S(1)} %broadcast_select_fusion.4), channel_id=1, source_target_pairs={{0,32},{32,64},{64,96},{96,128},{128,160},{160,192},{192,224},{224... | collective-permute-start | bytes 786440 | tf_op jit(solution)/shard_map/while/body/eval_jaxpr/ppermute | solution.py:10
  740.9 10.9 %collective-permute-start = (f32[8,32,256]{2,1,0:T(8,128)S(1)}, f32[8,32,256]{2,1,0:T(8,128)S(1)}, u32[]{:S(2)}, u32[]{:S(2)}) collective-permute-start(f32[8,32,256]{2,1,0:T(8,128)S(1)} %broadcast_select_fusion.4), channel_id=1, source_target_pairs={{0,32},{32,64},{64,96},{96,128},{128,160},{160,192},{192,224},{224... | collective-permute-start | bytes 786440 | tf_op jit(solution)/shard_map/while/body/eval_jaxpr/ppermute | solution.py:10
  752.2 12.0 %collective-permute-start = (f32[8,32,256]{2,1,0:T(8,128)S(1)}, f32[8,32,256]{2,1,0:T(8,128)S(1)}, u32[]{:S(2)}, u32[]{:S(2)}) collective-permute-start(f32[8,32,256]{2,1,0:T(8,128)S(1)} %broadcast_select_fusion.4), channel_id=1, source_target_pairs={{0,32},{32,64},{64,96},{96,128},{128,160},{160,192},{192,224},{224... | collective-permute-start | bytes 786440 | tf_op jit(solution)/shard_map/while/body/eval_jaxpr/ppermute | solution.py:10
  764.7 13.1 %collective-permute-start = (f32[8,32,256]{2,1,0:T(8,128)S(1)}, f32[8,32,256]{2,1,0:T(8,128)S(1)}, u32[]{:S(2)}, u32[]{:S(2)}) collective-permute-start(f32[8,32,256]{2,1,0:T(8,128)S(1)} %broadcast_select_fusion.4), channel_id=1, source_target_pairs={{0,32},{32,64},{64,96},{96,128},{128,160},{160,192},{192,224},{224... | collective-permute-start | bytes 786440 | tf_op jit(solution)/shard_map/while/body/eval_jaxpr/ppermute | solution.py:10
  778.4 12.3 %collective-permute-start = (f32[8,32,256]{2,1,0:T(8,128)S(1)}, f32[8,32,256]{2,1,0:T(8,128)S(1)}, u32[]{:S(2)}, u32[]{:S(2)}) collective-permute-start(f32[8,32,256]{2,1,0:T(8,128)S(1)} %broadcast_select_fusion.4), channel_id=1, source_target_pairs={{0,32},{32,64},{64,96},{96,128},{128,160},{160,192},{192,224},{224... | collective-permute-start | bytes 786440 | tf_op jit(solution)/shard_map/while/body/eval_jaxpr/ppermute | solution.py:10
  791.2 11.5 %collective-permute-start = (f32[8,32,256]{2,1,0:T(8,128)S(1)}, f32[8,32,256]{2,1,0:T(8,128)S(1)}, u32[]{:S(2)}, u32[]{:S(2)}) collective-permute-start(f32[8,32,256]{2,1,0:T(8,128)S(1)} %broadcast_select_fusion.4), channel_id=1, source_target_pairs={{0,32},{32,64},{64,96},{96,128},{128,160},{160,192},{192,224},{224... | collective-permute-start | bytes 786440 | tf_op jit(solution)/shard_map/while/body/eval_jaxpr/ppermute | solution.py:10
  803.2 10.6 %collective-permute-start = (f32[8,32,256]{2,1,0:T(8,128)S(1)}, f32[8,32,256]{2,1,0:T(8,128)S(1)}, u32[]{:S(2)}, u32[]{:S(2)}) collective-permute-start(f32[8,32,256]{2,1,0:T(8,128)S(1)} %broadcast_select_fusion.4), channel_id=1, source_target_pairs={{0,32},{32,64},{64,96},{96,128},{128,160},{160,192},{192,224},{224... | collective-permute-start | bytes 786440 | tf_op jit(solution)/shard_map/while/body/eval_jaxpr/ppermute | solution.py:10
  814.2 10.4 %collective-permute-start = (f32[8,32,256]{2,1,0:T(8,128)S(1)}, f32[8,32,256]{2,1,0:T(8,128)S(1)}, u32[]{:S(2)}, u32[]{:S(2)}) collective-permute-start(f32[8,32,256]{2,1,0:T(8,128)S(1)} %broadcast_select_fusion.4), channel_id=1, source_target_pairs={{0,32},{32,64},{64,96},{96,128},{128,160},{160,192},{192,224},{224... | collective-permute-start | bytes 786440 | tf_op jit(solution)/shard_map/while/body/eval_jaxpr/ppermute | solution.py:10
  825.1 10.4 %collective-permute-start = (f32[8,32,256]{2,1,0:T(8,128)S(1)}, f32[8,32,256]{2,1,0:T(8,128)S(1)}, u32[]{:S(2)}, u32[]{:S(2)}) collective-permute-start(f32[8,32,256]{2,1,0:T(8,128)S(1)} %broadcast_select_fusion.4), channel_id=1, source_target_pairs={{0,32},{32,64},{64,96},{96,128},{128,160},{160,192},{192,224},{224... | collective-permute-start | bytes 786440 | tf_op jit(solution)/shard_map/while/body/eval_jaxpr/ppermute | solution.py:10
  836.0 10.4 %collective-permute-start = (f32[8,32,256]{2,1,0:T(8,128)S(1)}, f32[8,32,256]{2,1,0:T(8,128)S(1)}, u32[]{:S(2)}, u32[]{:S(2)}) collective-permute-start(f32[8,32,256]{2,1,0:T(8,128)S(1)} %broadcast_select_fusion.4), channel_id=1, source_target_pairs={{0,32},{32,64},{64,96},{96,128},{128,160},{160,192},{192,224},{224... | collective-permute-start | bytes 786440 | tf_op jit(solution)/shard_map/while/body/eval_jaxpr/ppermute | solution.py:10
  846.9 10.4 %collective-permute-start = (f32[8,32,256]{2,1,0:T(8,128)S(1)}, f32[8,32,256]{2,1,0:T(8,128)S(1)}, u32[]{:S(2)}, u32[]{:S(2)}) collective-permute-start(f32[8,32,256]{2,1,0:T(8,128)S(1)} %broadcast_select_fusion.4), channel_id=1, source_target_pairs={{0,32},{32,64},{64,96},{96,128},{128,160},{160,192},{192,224},{224... | collective-permute-start | bytes 786440 | tf_op jit(solution)/shard_map/while/body/eval_jaxpr/ppermute | solution.py:10
where the time goes:
time: 866 us; the launch traced here: 862 us
  waiting for transfers between devices  514 us (59%)
  local copies, waits for them, and re-layouts  235 us (27%)
  starting transfers between devices  38.6 us (4%)
  other arithmetic  30 us (3%)
  blocking collectives  28.3 us (3%)
  matrix products  14.9 us (2%)
    all_to_all x1, waiting for transfers between devices, body(): lax.all_to_all(found_rows, 'tile', split_axis=0, concat_axis=0, tiled=True)  370 us
    ppermute x16, waiting for transfers between devices, from_behind(): lax.ppermute(value, axis, [(source, source + steps) for source in range(i...  144 us
    gather x1, local copies, waits for them, and re-layouts, body(): values = answers[owners, slot_of]  138 us
    gather x1, local copies, waits for them, and re-layouts, body(): jnp.take(local_pool, lax.all_to_all(requests, 'tile', split_axis=0, conca...  64.8 us
    ppermute x16, starting transfers between devices, from_behind(): lax.ppermute(value, axis, [(source, source + steps) for source in range(i...  32.4 us
    unnamed x25, local copies, waits for them, and re-layouts  31.9 us
    all_to_all x1, blocking collectives, body(): lax.all_to_all(requests, 'tile', split_axis=0, concat_axis=0, tiled=True)  28.3 us
    another operation x2, other arithmetic  17.3 us
  transfers between devices with their start and end apart: 17, of which 17 were waited for; matrix products, arithmetic and copies ran while one was open for 0% of the time, Pallas kernels for 0%

commit v1 on v0

v1 whole, which is shorter than its diff:
```python
import functools

import jax
import jax.numpy as jnp
from jax import lax
from jax.experimental import pallas as pl
from jax.experimental.pallas import tpu as pltpu
from jax.sharding import PartitionSpec as P

LANES = 128
UNROLL = 16
PIECES = 8
HIGHEST = lax.Precision.HIGHEST


def gather_kernel(
    pair_ref, count_ref, pool_hbm, live_ref, weight_ref, noise_ref, draw_ref,
    local_ref, edge_ref, pool, values, sems,
):
    blocks, entries = pair_ref.shape
    halves, edge = pool.shape[1], edge_ref.shape[1]
    cells = weight_ref.shape[0]
    rows = pool.shape[0] // PIECES
    copies = [
        pltpu.make_async_copy(
            pool_hbm.at[pl.ds(i * rows, rows)], pool.at[pl.ds(i * rows, rows)], sems.at[i]
        )
        for i in range(PIECES)
    ]
    for copy in copies:
        copy.start()
    values[...] = jnp.zeros_like(values)
    for b in range(blocks):
        local_ref[b] = jnp.dot(
            noise_ref[...], draw_ref[b], preferred_element_type=jnp.float32
        )
    for copy in copies:
        copy.wait()

    def block(b, _):
        def some(i, _):
            base = pl.multiple_of(i * UNROLL, UNROLL)
            places = [pair_ref[b, base + u] for u in range(UNROLL)]
            found = [[pool[p, h] for p in places] for h in range(halves)]
            for h in range(halves):
                for u in range(UNROLL):
                    values[h, base + u] = found[h][u]
            return 0

        lax.fori_loop(0, (count_ref[b] + UNROLL - 1) // UNROLL, some, 0)
        listed = jnp.concatenate(
            [values.at[h].reshape(2 * entries, LANES)[...] for h in range(halves)], axis=1
        )
        total = local_ref[b] + jnp.dot(
            weight_ref[...] * live_ref[b], listed, preferred_element_type=jnp.float32
        )
        local_ref[b] = total
        for h in range(halves):
            edge_ref[halves * b + h] = total[cells - edge :, h * LANES : (h + 1) * LANES]
        return 0

    lax.fori_loop(0, blocks, block, 0)


def gather_call(pair, count, pool, live, weight2, lower, draw, edge):
    blocks, entries = pair.shape
    cells, realizations = draw.shape[1:]
    halves = pool.shape[1]
    smem = pl.BlockSpec(memory_space=pltpu.SMEM)
    vmem = pl.BlockSpec(memory_space=pltpu.VMEM)
    return pl.pallas_call(
        gather_kernel,
        out_shape=(
            jax.ShapeDtypeStruct((blocks, cells, realizations), jnp.float32),
            jax.ShapeDtypeStruct((blocks * halves, edge, LANES), jnp.float32),
        ),
        in_specs=[smem, smem, pl.BlockSpec(memory_space=pl.ANY), vmem, vmem, vmem, vmem],
        out_specs=(vmem, vmem),
        scratch_shapes=[
            pltpu.VMEM(pool.shape, pool.dtype),
            pltpu.VMEM((halves, entries, 2, LANES), pool.dtype),
            pltpu.SemaphoreType.DMA((PIECES,)),
        ],
        compiler_params=pltpu.CompilerParams(vmem_limit_bytes=50 * 2**20),
        cost_estimate=pl.CostEstimate(
            flops=2 * blocks * cells * (2 * entries + cells) * realizations,
            bytes_accessed=5 * 2**24,
            transcendentals=0,
        ),
        name="gather",
    )(pair, count, pool, live, weight2, lower, draw)


def scan_kernel(scan_ref, face_ref, out_ref):
    out_ref[...] = jnp.dot(
        scan_ref[...], face_ref[...], precision=HIGHEST, preferred_element_type=jnp.float32
    )


def scan_call(scan, face):
    return pl.pallas_call(
        scan_kernel,
        out_shape=jax.ShapeDtypeStruct(face.shape, face.dtype),
        compiler_params=pltpu.CompilerParams(vmem_limit_bytes=16 * 2**20),
        name="scan",
    )(scan, face)


def finish_kernel(local_ref, face_ref, below_ref, out_ref):
    halves = local_ref.shape[2] // LANES
    for b in range(local_ref.shape[0]):
        below = jnp.concatenate([below_ref[halves * b + h] for h in range(halves)], axis=1)
        state = local_ref[b] + jnp.dot(
            face_ref[...], below, precision=HIGHEST, preferred_element_type=jnp.float32
        )
        out_ref[b] = state.astype(out_ref.dtype)


def finish_call(local, face, below):
    return pl.pallas_call(
        finish_kernel,
        out_shape=jax.ShapeDtypeStruct(local.shape, jnp.bfloat16),
        compiler_params=pltpu.CompilerParams(vmem_limit_bytes=16 * 2**20),
        name="finish",
    )(local, face, below)


def scan_matrix(square, count):
    edge = square.shape[0]
    mm = functools.partial(jnp.dot, precision=HIGHEST)
    powers = jnp.concatenate([square, jnp.eye(edge, dtype=square.dtype)], axis=1)
    top = mm(square, square)
    while powers.shape[1] < count * edge:
        powers = jnp.concatenate([mm(top, powers), powers], axis=1)
        top = mm(top, top)
    powers = powers[:, -(count - 1) * edge :]
    strip = jnp.concatenate([powers, jnp.zeros((edge, count * edge), powers.dtype)], axis=1)
    starts = [(count - 1 - f) * edge for f in range(count)]
    return jnp.concatenate([strip[:, s : s + count * edge] for s in starts])


def body(
    pool, nbr_owner, nbr_row, nbr_count, normal_draw, kriging_weight, noise_factor, face_weight
):
    pool_rows, realizations = pool.shape[1:]
    entries = nbr_row.shape[2]
    edge = face_weight.shape[1]
    halves = realizations // LANES
    front_count = lax.axis_size("front")
    mine = pool[0].reshape(pool_rows // 2, 2, halves, LANES).transpose(0, 2, 1, 3)
    gathered = lax.all_gather(mine, "tile", tiled=True)
    index = nbr_owner[0, :, :, 0] * pool_rows + nbr_row[0]
    pair = index >> 1
    count = nbr_count[0]
    is_live = jnp.arange(entries)[None, :] < count[:, None]
    live = (index & 1)[:, :, None] == jnp.arange(2)[None, None, :]
    live = (live & is_live[:, :, None]).astype(jnp.bfloat16).reshape(-1, 1, 2 * entries)
    weight2 = jnp.repeat(kriging_weight, 2, axis=1)
    scan = scan_matrix(face_weight[-edge:], front_count)
    local, face = gather_call(
        pair, count, gathered, live, weight2, jnp.tril(noise_factor), normal_draw[0], edge
    )
    swap = functools.partial(
        lax.all_to_all, axis_name="front", split_axis=0, concat_axis=0, tiled=True
    )
    below = scan_call(scan, swap(face).reshape(-1, LANES)).reshape(face.shape)
    return finish_call(local, face_weight, swap(below))[None]


def solution(mesh):
    placed = (
        P("front", "tile", None),
        P("front", "tile", None, None),
        P("front", "tile", None),
        P("front", "tile"),
        P("front", "tile", None, None),
        P(),
        P(),
        P(),
    )
    return jax.shard_map(
        body, mesh=mesh, in_specs=placed, out_specs=P("front", "tile", None, None), check_vma=False
    )
```

time: 866 us -> 197 us (0.23)
  the two profiles are of different devices: /device:TPU:48 before, /device:TPU:1 now
where the time goes in v1:
time: 197 us; the launch traced here: 196 us
  waiting for transfers between devices  104 us (53%)
  Pallas kernels  34.8 us (18%)
  local copies, waits for them, and re-layouts  16.7 us (8%)
  between operations  13.6 us (7%)
  starting transfers between devices  11.2 us (6%)
  blocking collectives  11.2 us (6%)
  other arithmetic  3.45 us (2%)
    all_gather x1, waiting for transfers between devices, body(): gathered = lax.all_gather(mine, 'tile', tiled=True)  99 us
    pallas_call x1, Pallas kernels, gather_call(): pl.pallas_call(gather_kernel, out_shape=(jax.ShapeDtypeStruct((blocks, ce...  31 us
    all_to_all x1, blocking collectives, body(): return finish_call(local, face_weight, swap(below))[None]  11.2 us
    all_to_all x1, starting transfers between devices, body(): below = scan_call(scan, swap(face).reshape(-1, LANES)).reshape(face.shape)  11.2 us
    unnamed x27, local copies, waits for them, and re-layouts  6.96 us
    all_to_all x1, waiting for transfers between devices, body(): below = scan_call(scan, swap(face).reshape(-1, LANES)).reshape(face.shape)  5.14 us
  transfers between devices with their start and end apart: 2, of which 2 were waited for; matrix products, arithmetic and copies ran while one was open for 8% of the time, Pallas kernels for 0%

profile of v1, /device:TPU:1, one launch (start us, length us, event | category | flops | bytes accessed | tf_op | source)
XLA Modules:
  0.0 196.2 jit_solution(10212854406421590077)
XLA Ops:
  6.5 1.3 reshape_squeeze.3
  7.8 1.2 copy.31
  9.0 0.7 iota_compare_fusion
  9.7 0.5 and.25
  10.2 0.7 and.26
  10.9 1.8 copy.35
  12.7 0.8 broadcast_and_fusion
  13.7 0.4 eq.35
  14.0 0.9 copy.33
  15.0 0.3 eq.38
  15.3 1.2 copy.36
  16.5 0.5 broadcast_in_dim.17
  17.1 0.4 reshape.96
  17.5 0.6 copy.37.weight_ref
  18.2 0.9 copy.39.face_ref
  19.2 0.2 fusion.24
  19.5 0.2 fusion.28
  19.9 0.3 fusion.16
  21.1 0.9 fusion.noise_ref
  22.0 1.0 and_convert_fusion.live_ref
  23.0 99.0 %all-gather.2.cloned.1.call-done.pool_hbm = bf16[16384,2,2,128]{3,2,1,0:T(2,128)(2,1)} async-done(((bf16[512,2,2,128]{3,2,1,0:T(2,128)(2,1)}), bf16[16384,2,2,128]{3,2,1,0:T(2,128)(2,1)}) %all-gather.2.cloned.1.call-update) | async-done | bytes 16777232 | tf_op jit(solution)/shard_map/all_gather | solution.py:151
  122.0 31.0 %gather.1 = (f32[8,256,256]{2,1,0:T(8,128)}, f32[16,32,128]{2,1,0:T(8,128)S(1)}) custom-call(s32[8,1024]{1,0:T(8,128)S(1)} %get-tuple-element.10.pair_ref, s32[8]{0:T(128)S(1)} %bitcast.34, bf16[16384,2,2,128]{3,2,1,0:T(2,128)(2,1)} %all-gather.2.cloned.1.call-done.pool_hbm, bf16[8,1,2048]{2,1,0:T(2,128)(2,1)S(1)} %and_convert_fusion.live_ref, ...), custom_call_target="tpu_custom_call" | custom-call | flops 2415919104 | bytes 83886080 | tf_op jit(solution)/shard_map/gather/pallas_call | solution.py:71
  153.1 0.7 copy-done.2
  153.8 11.2 %all-to-all-start = ((f32[16,32,128]{2,1,0:T(8,128)}), f32[16,32,128]{2,1,0:T(8,128)S(1)}, u32[]{:S(2)}, u32[]{:S(2)}) async-start(f32[16,32,128]{2,1,0:T(8,128)} %copy-done.2), calls=%async_computation | async-start | bytes 524288 | tf_op jit(solution)/shard_map/all_to_all | solution.py:166
  165.0 0.9 fusion.13
  165.9 0.9 fusion.14
  166.8 0.9 fusion.15.scan_ref
  167.7 5.1 %all-to-all-done = f32[16,32,128]{2,1,0:T(8,128)S(1)} async-done(((f32[16,32,128]{2,1,0:T(8,128)}), f32[16,32,128]{2,1,0:T(8,128)S(1)}, u32[]{:S(2)}, u32[]{:S(2)}) %all-to-all-start) | async-done | bytes 262176 | tf_op jit(solution)/shard_map/all_to_all | solution.py:166
  172.8 1.0 scan.1
  173.8 11.2 %all_to_all.10.below_ref = f32[16,32,128]{2,1,0:T(8,128)S(1)} all-to-all(f32[16,32,128]{2,1,0:T(8,128)S(1)} %bitcast.32), channel_id=1, replica_groups=mesh['front'=16,'tile'=32] {'front'}, dimensions={0} | all-to-all | bytes 524288 | tf_op jit(solution)/shard_map/all_to_all | solution.py:167
  185.0 1.6 copy-done
  186.6 2.7 %finish.1 = bf16[8,256,256]{2,1,0:T(8,128)(2,1)} custom-call(f32[8,256,256]{2,1,0:T(8,128)S(1)} %copy-done, f32[256,32]{1,0:T(8,128)S(1)} %copy.39.face_ref, f32[16,32,128]{2,1,0:T(8,128)S(1)} %all_to_all.10.below_ref), custom_call_target="tpu_custom_call" | custom-call | tf_op jit(solution)/shard_map/finish/pallas_call | solution.py:120
  (32 shorter events, 1.6 us)
Async XLA Ops:
  6.5 115.5 %copy-start.3 = (s32[1,8]{1,0:T(1,128)S(1)}, s32[1,8]{1,0:T(1,128)}, u32[]{:S(2)}) copy-start(s32[1,8]{1,0:T(1,128)} %param.11) | copy-start | bytes 100
  6.5 115.5 %copy-start.1 = (bf16[1,8,256,256]{3,2,1,0:T(8,128)(2,1)S(1)}, bf16[1,8,256,256]{3,2,1,0:T(8,128)(2,1)}, u32[]{:S(2)}) copy-start(bf16[1,8,256,256]{3,2,1,0:T(8,128)(2,1)} %param.12) | copy-start | bytes 3145732
  6.5 115.5 %all-gather.2.cloned.1.call-start = ((), (), s32[]{:S(2)}) async-start(), calls=%async_computation.2 | async-start | bytes 17301504 | tf_op jit(solution)/shard_map/all_gather | solution.py:151
  20.3 0.8 copy-start.4
  153.1 0.7 copy-start.2
  153.8 19.0 %all-to-all-start = ((f32[16,32,128]{2,1,0:T(8,128)}), f32[16,32,128]{2,1,0:T(8,128)S(1)}, u32[]{:S(2)}, u32[]{:S(2)}) async-start(f32[16,32,128]{2,1,0:T(8,128)} %copy-done.2), calls=%async_computation | async-start | bytes 524288 | tf_op jit(solution)/shard_map/all_to_all | solution.py:166
  185.0 1.6 copy-start
Sparse Core Ops, SparseCore 0:
  9.5 112.4 all-gather.1

commit v2 on v1

--- a/solution.py
+++ b/solution.py
@@ -8,18 +8,19 @@
 from jax.sharding import PartitionSpec as P
 
 LANES = 128
-UNROLL = 16
+UNROLL = 32
 PIECES = 8
+PAIRS = 4
 HIGHEST = lax.Precision.HIGHEST
 
 
 def gather_kernel(
-    pair_ref, count_ref, pool_hbm, live_ref, weight_ref, noise_ref, draw_ref,
+    tile_ref, count_ref, pool_hbm, live_ref, weight_ref, noise_ref, draw_ref,
     local_ref, edge_ref, pool, values, sems,
 ):
-    blocks, entries = pair_ref.shape
-    halves, edge = pool.shape[1], edge_ref.shape[1]
-    cells = weight_ref.shape[0]
+    blocks, cells, realizations = local_ref.shape
+    halves, entries = values.shape[:2]
+    edge = edge_ref.shape[1]
     rows = pool.shape[0] // PIECES
     copies = [
         pltpu.make_async_copy(
@@ -40,8 +41,8 @@
     def block(b, _):
         def some(i, _):
             base = pl.multiple_of(i * UNROLL, UNROLL)
-            places = [pair_ref[b, base + u] for u in range(UNROLL)]
-            found = [[pool[p, h] for p in places] for h in range(halves)]
+            places = [tile_ref[b * entries + base + u] for u in range(UNROLL)]
+            found = [[pool[p + h * PAIRS] for p in places] for h in range(halves)]
             for h in range(halves):
                 for u in range(UNROLL):
                     values[h, base + u] = found[h][u]
@@ -62,10 +63,10 @@
     lax.fori_loop(0, blocks, block, 0)
 
 
-def gather_call(pair, count, pool, live, weight2, lower, draw, edge):
-    blocks, entries = pair.shape
-    cells, realizations = draw.shape[1:]
-    halves = pool.shape[1]
+def gather_call(tile, count, pool, live, weight2, lower, draw, edge):
+    blocks, cells, realizations = draw.shape
+    halves = realizations // LANES
+    entries = tile.shape[0] // blocks
     smem = pl.BlockSpec(memory_space=pltpu.SMEM)
     vmem = pl.BlockSpec(memory_space=pltpu.VMEM)
     return pl.pallas_call(
@@ -88,7 +89,7 @@
             transcendentals=0,
         ),
         name="gather",
-    )(pair, count, pool, live, weight2, lower, draw)
+    )(tile, count, pool, live, weight2, lower, draw)
 
 
 def scan_kernel(scan_ref, face_ref, out_ref):
@@ -107,20 +108,29 @@
 
 
 def finish_kernel(local_ref, face_ref, below_ref, out_ref):
-    halves = local_ref.shape[2] // LANES
-    for b in range(local_ref.shape[0]):
-        below = jnp.concatenate([below_ref[halves * b + h] for h in range(halves)], axis=1)
-        state = local_ref[b] + jnp.dot(
-            face_ref[...], below, precision=HIGHEST, preferred_element_type=jnp.float32
-        )
-        out_ref[b] = state.astype(out_ref.dtype)
+    halves = below_ref.shape[0]
+    below = jnp.concatenate([below_ref[h] for h in range(halves)], axis=1)
+    state = local_ref[0] + jnp.dot(
+        face_ref[...], below, precision=HIGHEST, preferred_element_type=jnp.float32
+    )
+    out_ref[0] = state.astype(out_ref.dtype)
 
 
 def finish_call(local, face, below):
+    blocks, cells, realizations = local.shape
+    edge = face.shape[1]
+    halves = realizations // LANES
+    whole = pl.BlockSpec((1, cells, realizations), lambda b: (b, 0, 0))
     return pl.pallas_call(
         finish_kernel,
+        grid=(blocks,),
         out_shape=jax.ShapeDtypeStruct(local.shape, jnp.bfloat16),
-        compiler_params=pltpu.CompilerParams(vmem_limit_bytes=16 * 2**20),
+        in_specs=[
+            whole,
+            pl.BlockSpec((cells, edge), lambda b: (0, 0)),
+            pl.BlockSpec((halves, edge, LANES), lambda b: (b, 0, 0)),
+        ],
+        out_specs=whole,
         name="finish",
     )(local, face, below)
 
@@ -147,10 +157,12 @@
     edge = face_weight.shape[1]
     halves = realizations // LANES
     front_count = lax.axis_size("front")
-    mine = pool[0].reshape(pool_rows // 2, 2, halves, LANES).transpose(0, 2, 1, 3)
-    gathered = lax.all_gather(mine, "tile", tiled=True)
+    group = 2 * PAIRS
+    gathered = lax.all_gather(pool[0], "tile", tiled=True)
+    pieces = gathered.reshape(-1, PAIRS, 2, halves, LANES).transpose(0, 3, 1, 2, 4)
+    pieces = pieces.reshape(-1, 2, LANES)
     index = nbr_owner[0, :, :, 0] * pool_rows + nbr_row[0]
-    pair = index >> 1
+    tile = index // group * (halves * PAIRS) + index % group // 2
     count = nbr_count[0]
     is_live = jnp.arange(entries)[None, :] < count[:, None]
     live = (index & 1)[:, :, None] == jnp.arange(2)[None, None, :]
@@ -158,7 +170,7 @@
     weight2 = jnp.repeat(kriging_weight, 2, axis=1)
     scan = scan_matrix(face_weight[-edge:], front_count)
     local, face = gather_call(
-        pair, count, gathered, live, weight2, jnp.tril(noise_factor), normal_draw[0], edge
+        tile.reshape(-1), count, pieces, live, weight2, jnp.tril(noise_factor), normal_draw[0], edge
     )
     swap = functools.partial(
         lax.all_to_all, axis_name="front", split_axis=0, concat_axis=0, tiled=True

time: 197 us -> 186 us (0.944)
  local copies, waits for them, and re-layouts: 16.7 us -> 9.61 us
  Pallas kernels: 34.8 us -> 29.9 us
  starting transfers between devices: 11.2 us -> 7.02 us
  waiting for transfers between devices: 104 us -> 108 us
    pallas_call x1, Pallas kernels: 31 us -> 22.1 us  [gather_call(): pl.pallas_call(gather_kernel, out_shape=(jax.ShapeDtypeStruct((blocks, ce...]
    all_to_all x1, starting transfers between devices: 11.2 us -> 7.02 us  [body(): below = scan_call(scan, swap(face).reshape(-1, LANES)).reshape(face.shape)]
    pallas_call x1, Pallas kernels: 2.74 us -> 6.77 us  [finish_call(): pl.pallas_call(finish_kernel, grid=(blocks,), out_shape=jax.ShapeDtypeStr...]
    unnamed x27 -> x25, local copies, waits for them, and re-layouts: 6.96 us -> 3.69 us
    all_to_all x1, waiting for transfers between devices: 5.14 us -> 7.97 us  [body(): below = scan_call(scan, swap(face).reshape(-1, LANES)).reshape(face.shape)]
where the time goes in v2:
time: 186 us; the launch traced here: 185 us
  waiting for transfers between devices  108 us (58%)
  Pallas kernels  29.9 us (16%)
  between operations  13.6 us (7%)
  blocking collectives  10.8 us (6%)
  local copies, waits for them, and re-layouts  9.61 us (5%)
  starting transfers between devices  7.02 us (4%)
  other arithmetic  5.02 us (3%)
    all_gather x1, waiting for transfers between devices, body(): gathered = lax.all_gather(pool[0], 'tile', tiled=True)  99.7 us
    pallas_call x1, Pallas kernels, gather_call(): pl.pallas_call(gather_kernel, out_shape=(jax.ShapeDtypeStruct((blocks, ce...  22.1 us
    all_to_all x1, blocking collectives, body(): return finish_call(local, face_weight, swap(below))[None]  10.8 us
    all_to_all x1, waiting for transfers between devices, body(): below = scan_call(scan, swap(face).reshape(-1, LANES)).reshape(face.shape)  7.97 us
    all_to_all x1, starting transfers between devices, body(): below = scan_call(scan, swap(face).reshape(-1, LANES)).reshape(face.shape)  7.02 us
    pallas_call x1, Pallas kernels, finish_call(): pl.pallas_call(finish_kernel, grid=(blocks,), out_shape=jax.ShapeDtypeStr...  6.77 us
  transfers between devices with their start and end apart: 2, of which 2 were waited for; matrix products, arithmetic and copies ran while one was open for 8% of the time, Pallas kernels for 0%

profile of v2, /device:TPU:1, one launch (start us, length us, event | category | flops | bytes accessed | tf_op | source)
XLA Modules:
  0.0 185.5 jit_solution(8324071905506525147)
XLA Ops:
  6.5 0.7 all-gather.3.cloned.1.call-update
  7.3 0.7 iota_compare_fusion
  8.0 0.5 and.48
  8.5 0.7 and.49
  9.2 1.2 copy.27
  10.3 0.8 fusion.27
  11.1 0.2 copy.24
  11.3 0.4 eq.37
  11.7 0.9 copy.25
  12.7 0.3 eq.40
  13.0 1.2 copy.28
  14.2 0.5 broadcast_in_dim.17
  14.8 0.4 reshape.109
  15.2 0.6 copy.29.weight_ref
  15.9 0.9 copy.31.face_ref
  16.9 0.2 fusion.32
  17.1 0.1 fusion.48
  17.2 0.2 fusion.36
  17.5 0.1 fusion.49
  17.6 0.3 fusion.19
  18.8 0.8 fusion.31
  19.6 0.8 fusion.17.tile_ref
  20.4 0.9 fusion.noise_ref
  21.3 0.9 and_convert_fusion.live_ref
  22.3 99.7 %all-gather.3.cloned.1.call-done = bf16[1,32768,256]{2,1,0:T(8,128)(2,1)} async-done(((bf16[1,1024,256]{2,1,0:T(8,128)(2,1)}), bf16[1,32768,256]{2,1,0:T(8,128)(2,1)}) %all-gather.3.cloned.1.call-update) | async-done | bytes 16777232 | tf_op jit(solution)/shard_map/all_gather | solution.py:161
  122.0 22.1 %gather.1 = (f32[8,256,256]{2,1,0:T(8,128)}, f32[16,32,128]{2,1,0:T(8,128)S(1)}) custom-call(s32[8192]{0:T(1024)S(1)} %fusion.17.tile_ref, s32[8]{0:T(128)S(1)} %bitcast.44, bf16[32768,2,128]{2,1,0:T(2,128)(2,1)} %bitcast.45, bf16[8,1,2048]{2,1,0:T(2,128)(2,1)S(1)} %and_convert_fusion.live_ref, bf16[256,2048]{1,0:T(8,128)(2,1)S(1)} %copy.29.weight_ref, ...), custom_call_target="tpu_custom_call" | custom-call | flops 2415919104 | bytes 83886080 | tf_op jit(solution)/shard_map/gather/pallas_call | solution.py:72
  144.1 0.7 copy-done.1
  144.8 7.0 %all-to-all-start = ((f32[16,32,128]{2,1,0:T(8,128)}), f32[16,32,128]{2,1,0:T(8,128)S(1)}, u32[]{:S(2)}, u32[]{:S(2)}) async-start(f32[16,32,128]{2,1,0:T(8,128)} %copy-done.1), calls=%async_computation | async-start | bytes 524288 | tf_op jit(solution)/shard_map/all_to_all | solution.py:178
  152.0 8.0 %all-to-all-done = f32[16,32,128]{2,1,0:T(8,128)S(1)} async-done(((f32[16,32,128]{2,1,0:T(8,128)}), f32[16,32,128]{2,1,0:T(8,128)S(1)}, u32[]{:S(2)}, u32[]{:S(2)}) %all-to-all-start) | async-done | bytes 262176 | tf_op jit(solution)/shard_map/all_to_all | solution.py:178
  160.0 1.0 scan.1
  161.0 10.8 %all_to_all.10.below_ref = f32[16,32,128]{2,1,0:T(8,128)} all-to-all(f32[16,32,128]{2,1,0:T(8,128)S(1)} %bitcast.42), channel_id=1, replica_groups=mesh['front'=16,'tile'=32] {'front'}, dimensions={0} | all-to-all | bytes 524288 | tf_op jit(solution)/shard_map/all_to_all | solution.py:179
  171.9 6.8 %finish.1 = bf16[8,256,256]{2,1,0:T(8,128)(2,1)} custom-call(f32[8,256,256]{2,1,0:T(8,128)} %get-tuple-element.7.local_ref, f32[256,32]{1,0:T(8,128)} %copy-done.3, f32[16,32,128]{2,1,0:T(8,128)} %all_to_all.10.below_ref), custom_call_target="tpu_custom_call" | custom-call | tf_op jit(solution)/shard_map/finish/pallas_call | solution.py:124
  (30 shorter events, 1.3 us)
Async XLA Ops:
  6.5 115.5 %copy-start.2 = (s32[1,8]{1,0:T(1,128)S(1)}, s32[1,8]{1,0:T(1,128)}, u32[]{:S(2)}) copy-start(s32[1,8]{1,0:T(1,128)} %param.11) | copy-start | bytes 100
  6.5 115.5 %copy-start = (bf16[1,8,256,256]{3,2,1,0:T(8,128)(2,1)S(1)}, bf16[1,8,256,256]{3,2,1,0:T(8,128)(2,1)}, u32[]{:S(2)}) copy-start(bf16[1,8,256,256]{3,2,1,0:T(8,128)(2,1)} %param.12) | copy-start | bytes 3145732
  6.5 115.5 %all-gather.3.cloned.1.call-start = ((), (), s32[]{:S(2)}) async-start(), calls=%async_computation.2 | async-start | bytes 17301504 | tf_op jit(solution)/shard_map/all_gather | solution.py:161
  16.7 1.3 copy-start.3
  144.1 0.7 copy-start.1
  144.8 15.2 %all-to-all-start = ((f32[16,32,128]{2,1,0:T(8,128)}), f32[16,32,128]{2,1,0:T(8,128)S(1)}, u32[]{:S(2)}, u32[]{:S(2)}) async-start(f32[16,32,128]{2,1,0:T(8,128)} %copy-done.1), calls=%async_computation | async-start | bytes 524288 | tf_op jit(solution)/shard_map/all_to_all | solution.py:178
Sparse Core Ops, SparseCore 0:
  9.5 112.4 all-gather.2

commit v3 on v2

--- a/solution.py
+++ b/solution.py
@@ -11,23 +11,31 @@
 UNROLL = 32
 PIECES = 8
 PAIRS = 4
+REST = 320
+SCALE = 2.0**13
+FINISH_BLOCKS = 4
 HIGHEST = lax.Precision.HIGHEST
 
 
 def gather_kernel(
-    tile_ref, count_ref, pool_hbm, live_ref, weight_ref, noise_ref, draw_ref,
+    tile_ref, count_ref, main_hbm, rest_hbm, live_ref, weight_ref, noise_ref, draw_ref,
     local_ref, edge_ref, pool, values, sems,
 ):
     blocks, cells, realizations = local_ref.shape
     halves, entries = values.shape[:2]
     edge = edge_ref.shape[1]
-    rows = pool.shape[0] // PIECES
-    copies = [
-        pltpu.make_async_copy(
-            pool_hbm.at[pl.ds(i * rows, rows)], pool.at[pl.ds(i * rows, rows)], sems.at[i]
-        )
-        for i in range(PIECES)
-    ]
+    copies, start = [], 0
+    for source in (rest_hbm, main_hbm):
+        rows = source.shape[0] // PIECES
+        for i in range(PIECES):
+            copies.append(
+                pltpu.make_async_copy(
+                    source.at[pl.ds(i * rows, rows)],
+                    pool.at[pl.ds(start + i * rows, rows)],
+                    sems.at[len(copies)],
+                )
+            )
+        start += source.shape[0]
     for copy in copies:
         copy.start()
     values[...] = jnp.zeros_like(values)
@@ -63,24 +71,25 @@
     lax.fori_loop(0, blocks, block, 0)
 
 
-def gather_call(tile, count, pool, live, weight2, lower, draw, edge):
+def gather_call(tile, count, main, rest, live, weight2, lower, draw, edge):
     blocks, cells, realizations = draw.shape
     halves = realizations // LANES
     entries = tile.shape[0] // blocks
     smem = pl.BlockSpec(memory_space=pltpu.SMEM)
     vmem = pl.BlockSpec(memory_space=pltpu.VMEM)
+    hbm = pl.BlockSpec(memory_space=pl.ANY)
     return pl.pallas_call(
         gather_kernel,
         out_shape=(
             jax.ShapeDtypeStruct((blocks, cells, realizations), jnp.float32),
             jax.ShapeDtypeStruct((blocks * halves, edge, LANES), jnp.float32),
         ),
-        in_specs=[smem, smem, pl.BlockSpec(memory_space=pl.ANY), vmem, vmem, vmem, vmem],
+        in_specs=[smem, smem, hbm, hbm, vmem, vmem, vmem, vmem],
         out_specs=(vmem, vmem),
         scratch_shapes=[
-            pltpu.VMEM(pool.shape, pool.dtype),
-            pltpu.VMEM((halves, entries, 2, LANES), pool.dtype),
-            pltpu.SemaphoreType.DMA((PIECES,)),
+            pltpu.VMEM((main.shape[0] + rest.shape[0], 2, LANES), main.dtype),
+            pltpu.VMEM((halves, entries, 2, LANES), main.dtype),
+            pltpu.SemaphoreType.DMA((2 * PIECES,)),
         ],
         compiler_params=pltpu.CompilerParams(vmem_limit_bytes=50 * 2**20),
         cost_estimate=pl.CostEstimate(
@@ -89,7 +98,7 @@
             transcendentals=0,
         ),
         name="gather",
-    )(tile, count, pool, live, weight2, lower, draw)
+    )(tile, count, main, rest, live, weight2, lower, draw)
 
 
 def scan_kernel(scan_ref, face_ref, out_ref):
@@ -108,27 +117,30 @@
 
 
 def finish_kernel(local_ref, face_ref, below_ref, out_ref):
-    halves = below_ref.shape[0]
-    below = jnp.concatenate([below_ref[h] for h in range(halves)], axis=1)
-    state = local_ref[0] + jnp.dot(
-        face_ref[...], below, precision=HIGHEST, preferred_element_type=jnp.float32
-    )
-    out_ref[0] = state.astype(out_ref.dtype)
+    blocks, _, realizations = local_ref.shape
+    halves = realizations // LANES
+    for b in range(blocks):
+        below = jnp.concatenate([below_ref[halves * b + h] for h in range(halves)], axis=1)
+        state = local_ref[b] + jnp.dot(
+            face_ref[...], below, precision=HIGHEST, preferred_element_type=jnp.float32
+        )
+        out_ref[b] = state.astype(out_ref.dtype)
 
 
 def finish_call(local, face, below):
     blocks, cells, realizations = local.shape
     edge = face.shape[1]
     halves = realizations // LANES
-    whole = pl.BlockSpec((1, cells, realizations), lambda b: (b, 0, 0))
+    size = FINISH_BLOCKS
+    whole = pl.BlockSpec((size, cells, realizations), lambda b: (b, 0, 0))
     return pl.pallas_call(
         finish_kernel,
-        grid=(blocks,),
+        grid=(blocks // size,),
         out_shape=jax.ShapeDtypeStruct(local.shape, jnp.bfloat16),
         in_specs=[
             whole,
             pl.BlockSpec((cells, edge), lambda b: (0, 0)),
-            pl.BlockSpec((halves, edge, LANES), lambda b: (b, 0, 0)),
+            pl.BlockSpec((size * halves, edge, LANES), lambda b: (b, 0, 0)),
         ],
         out_specs=whole,
         name="finish",
@@ -158,10 +170,23 @@
     halves = realizations // LANES
     front_count = lax.axis_size("front")
     group = 2 * PAIRS
-    gathered = lax.all_gather(pool[0], "tile", tiled=True)
-    pieces = gathered.reshape(-1, PAIRS, 2, halves, LANES).transpose(0, 3, 1, 2, 4)
-    pieces = pieces.reshape(-1, 2, LANES)
-    index = nbr_owner[0, :, :, 0] * pool_rows + nbr_row[0]
+    tiles = lax.axis_size("tile")
+
+    def as_pieces(rows):
+        rows = rows.reshape(-1, PAIRS, 2, halves, LANES).transpose(0, 3, 1, 2, 4)
+        return rows.reshape(-1, 2, LANES)
+
+    main_rows = pool_rows - REST
+    main = as_pieces(lax.all_gather(pool[0, :main_rows], "tile", tiled=True))
+    scaled = (pool[0, main_rows:] * SCALE).astype(jnp.float16)
+    rest = lax.all_gather(scaled, "tile", tiled=True)
+    rest = as_pieces(rest.astype(pool.dtype) * jnp.asarray(1 / SCALE, pool.dtype))
+    owner, row = nbr_owner[0, :, :, 0], nbr_row[0]
+    index = jnp.where(
+        row < main_rows,
+        tiles * REST + owner * main_rows + row,
+        owner * REST + row - main_rows,
+    )
     tile = index // group * (halves * PAIRS) + index % group // 2
     count = nbr_count[0]
     is_live = jnp.arange(entries)[None, :] < count[:, None]
@@ -170,7 +195,7 @@
     weight2 = jnp.repeat(kriging_weight, 2, axis=1)
     scan = scan_matrix(face_weight[-edge:], front_count)
     local, face = gather_call(
-        tile.reshape(-1), count, pieces, live, weight2, jnp.tril(noise_factor), normal_draw[0], edge
+        tile.reshape(-1), count, main, rest, live, weight2, jnp.tril(noise_factor), normal_draw[0], edge
     )
     swap = functools.partial(
         lax.all_to_all, axis_name="front", split_axis=0, concat_axis=0, tiled=True

time: 186 us -> 185 us (level)
  blocking collectives: 10.8 us -> 94.4 us
  waiting for transfers between devices: 108 us -> 24.6 us
  Pallas kernels: 29.9 us -> 26.9 us
    all_gather x0 -> x1, blocking collectives: none -> 83.5 us  [body(): rest = lax.all_gather(scaled, 'tile', tiled=True)]
    all_gather x1, waiting for transfers between devices: 99.7 us -> 16.2 us  [body(): main = as_pieces(lax.all_gather(pool[0, :main_rows], 'tile', tiled=True))]
    mul x0 -> x1, other arithmetic: none -> 2.77 us  [body(): rest.astype(pool.dtype) * jnp.asarray(1 / SCALE, pool.dtype)]
    pallas_call x1, Pallas kernels: 6.77 us -> 4.01 us  [finish_call(): pl.pallas_call(finish_kernel, grid=(blocks // size,), out_shape=jax.Shape...]
where the time goes in v3:
time: 185 us; the launch traced here: 184 us
  blocking collectives  94.4 us (51%)
  Pallas kernels  26.9 us (15%)
  waiting for transfers between devices  24.6 us (13%)
  between operations  13.7 us (7%)
  local copies, waits for them, and re-layouts  9.75 us (5%)
  starting transfers between devices  8.32 us (4%)
  other arithmetic  5.49 us (3%)
    all_gather x1, blocking collectives, body(): rest = lax.all_gather(scaled, 'tile', tiled=True)  83.5 us
    pallas_call x1, Pallas kernels, gather_call(): pl.pallas_call(gather_kernel, out_shape=(jax.ShapeDtypeStruct((blocks, ce...  21.8 us
    all_gather x1, waiting for transfers between devices, body(): main = as_pieces(lax.all_gather(pool[0, :main_rows], 'tile', tiled=True))  16.2 us
    all_to_all x1, blocking collectives, body(): return finish_call(local, face_weight, swap(below))[None]  10.8 us
    all_to_all x1, waiting for transfers between devices, body(): below = scan_call(scan, swap(face).reshape(-1, LANES)).reshape(face.shape)  8.35 us
    all_to_all x1, starting transfers between devices, body(): below = scan_call(scan, swap(face).reshape(-1, LANES)).reshape(face.shape)  8.32 us
    pallas_call x1, Pallas kernels, finish_call(): pl.pallas_call(finish_kernel, grid=(blocks // size,), out_shape=jax.Shape...  4.01 us
  transfers between devices with their start and end apart: 2, of which 2 were waited for; matrix products, arithmetic and copies ran while one was open for 8% of the time, Pallas kernels for 0%

profile of v3, /device:TPU:1, one launch (start us, length us, event | category | flops | bytes accessed | tf_op | source)
XLA Modules:
  0.0 184.2 jit_solution(1262559970303276875)
XLA Ops:
  6.5 1.8 slice.57
  8.4 0.9 copy.37.face_ref
  9.3 0.1 fusion.51
  9.4 0.2 fusion.37
  9.6 0.1 fusion.53
  9.8 0.2 fusion.41
  10.0 0.1 fusion.54
  10.1 0.3 fusion.21
  10.6 0.7 iota_compare_fusion
  11.3 0.5 and.48
  11.8 0.7 and.49
  12.5 1.2 copy.33
  13.6 0.8 fusion.31
  14.4 0.2 copy.30
  14.6 0.4 eq.37
  15.0 0.3 copy.31
  15.4 0.3 eq.40
  15.7 0.2 copy.34
  15.9 0.5 broadcast_in_dim.17
  16.4 0.4 reshape.143
  16.9 0.6 copy.35.weight_ref
  18.4 1.0 multiply_convert_fusion
  19.5 83.5 %all-gather.6 = f16[1,10240,256]{2,1,0:T(8,128)(2,1)S(1)} all-gather(f16[1,320,256]{2,1,0:T(8,128)(2,1)S(1)} %multiply_convert_fusion), channel_id=3, replica_groups=mesh['front'=16,'tile'=32] {'tile'}, dimensions={1}, use_global_device_ids=true | all-gather | bytes 5406720 | tf_op jit(solution)/shard_map/all_gather | solution.py:182
  103.1 2.8 %convert_multiply_fusion = bf16[1,10240,256]{2,1,0:T(8,128)(2,1)} fusion(f16[1,10240,256]{2,1,0:T(8,128)(2,1)S(1)} %all-gather.6), kind=kLoop, calls=%fused_computation | loop fusion | flops 5242880 | bytes 10485760 | tf_op jit(solution)/shard_map/mul | solution.py:183
  105.8 16.2 %all-gather.5.cloned.1.call-done = bf16[1,22528,256]{2,1,0:T(8,128)(2,1)} async-done(((bf16[1,704,256]{2,1,0:T(8,128)(2,1)}), bf16[1,22528,256]{2,1,0:T(8,128)(2,1)}) %all-gather.5.cloned.1.call-update) | async-done | bytes 11534352 | tf_op jit(solution)/shard_map/all_gather | solution.py:180
  122.1 21.8 %gather.1 = (f32[8,256,256]{2,1,0:T(8,128)}, f32[16,32,128]{2,1,0:T(8,128)S(1)}) custom-call(s32[8192]{0:T(1024)S(1)} %fusion.17.tile_ref, s32[8]{0:T(128)S(1)} %bitcast.76, bf16[22528,2,128]{2,1,0:T(2,128)(2,1)} %bitcast.78, bf16[10240,2,128]{2,1,0:T(2,128)(2,1)} %bitcast.77, bf16[8,1,2048]{2,1,0:T(2,128)(2,1)S(1)} %and_convert_fusion.live_ref, ...), custom_call_target="tpu_custom_call" | custom-call | flops 2415919104 | bytes 83886080 | tf_op jit(solution)/shard_map/gather/pallas_call | solution.py:81
  143.9 0.7 copy-done.1
  144.6 8.3 %all-to-all-start = ((f32[16,32,128]{2,1,0:T(8,128)}), f32[16,32,128]{2,1,0:T(8,128)S(1)}, u32[]{:S(2)}, u32[]{:S(2)}) async-start(f32[16,32,128]{2,1,0:T(8,128)} %copy-done.1), calls=%async_computation | async-start | bytes 524288 | tf_op jit(solution)/shard_map/all_to_all | solution.py:203
  153.1 8.4 %all-to-all-done = f32[16,32,128]{2,1,0:T(8,128)S(1)} async-done(((f32[16,32,128]{2,1,0:T(8,128)}), f32[16,32,128]{2,1,0:T(8,128)S(1)}, u32[]{:S(2)}, u32[]{:S(2)}) %all-to-all-start) | async-done | bytes 262176 | tf_op jit(solution)/shard_map/all_to_all | solution.py:203
  161.5 1.0 scan.1
  162.5 10.8 %all_to_all.10.below_ref = f32[16,32,128]{2,1,0:T(8,128)} all-to-all(f32[16,32,128]{2,1,0:T(8,128)S(1)} %bitcast.74), channel_id=1, replica_groups=mesh['front'=16,'tile'=32] {'front'}, dimensions={0} | all-to-all | bytes 524288 | tf_op jit(solution)/shard_map/all_to_all | solution.py:204
  173.3 4.0 %finish.1 = bf16[8,256,256]{2,1,0:T(8,128)(2,1)} custom-call(f32[8,256,256]{2,1,0:T(8,128)} %get-tuple-element.7.local_ref, f32[256,32]{1,0:T(8,128)} %copy-done.3, f32[16,32,128]{2,1,0:T(8,128)} %all_to_all.10.below_ref), custom_call_target="tpu_custom_call" | custom-call | tf_op jit(solution)/shard_map/finish/pallas_call | solution.py:136
  (42 shorter events, 1.4 us)
Async XLA Ops:
  6.5 9.1 %copy-start.4 = (bf16[256,1024]{1,0:T(8,128)(2,1)S(1)}, bf16[256,1024]{1,0:T(8,128)(2,1)}, u32[]{:S(2)}) copy-start(bf16[256,1024]{1,0:T(8,128)(2,1)} %param.13) | copy-start | bytes 1572868
  6.5 115.5 %all-gather.5.cloned.1.call-start = ((), (), s32[]{:S(2)}) async-start(), calls=%async_computation.2 | async-start | bytes 11894784 | tf_op jit(solution)/shard_map/all_gather | solution.py:180
  9.2 1.3 copy-start.3
  15.0 3.3 %copy-start.5 = (s32[1,8,1024,1]{2,3,1,0:T(1,128)S(1)}, s32[1,8,1024,1]{2,3,1,0:T(1,128)}, u32[]{:S(2)}) copy-start(s32[1,8,1024,1]{2,3,1,0:T(1,128)} %param.9) | copy-start | bytes 98308
  15.0 3.3 %copy-start.7 = (s32[1,8,1024]{2,1,0:T(8,128)S(1)}, s32[1,8,1024]{2,1,0:T(8,128)}, u32[]{:S(2)}) copy-start(s32[1,8,1024]{2,1,0:T(8,128)} %param.10) | copy-start | bytes 98308
  15.0 3.4 %copy-start.6 = (bf16[256,256]{1,0:T(8,128)(2,1)S(1)}, bf16[256,256]{1,0:T(8,128)(2,1)}, u32[]{:S(2)}) copy-start(bf16[256,256]{1,0:T(8,128)(2,1)} %param.14) | copy-start | bytes 393220
  103.0 19.0 %copy-start = (bf16[1,8,256,256]{3,2,1,0:T(8,128)(2,1)S(1)}, bf16[1,8,256,256]{3,2,1,0:T(8,128)(2,1)}, u32[]{:S(2)}) copy-start(bf16[1,8,256,256]{3,2,1,0:T(8,128)(2,1)} %param.12) | copy-start | bytes 3145732
  103.0 19.0 %copy-start.2 = (s32[1,8]{1,0:T(1,128)S(1)}, s32[1,8]{1,0:T(1,128)}, u32[]{:S(2)}) copy-start(s32[1,8]{1,0:T(1,128)} %param.11) | copy-start | bytes 100
  143.9 0.7 copy-start.1
  144.6 16.9 %all-to-all-start = ((f32[16,32,128]{2,1,0:T(8,128)}), f32[16,32,128]{2,1,0:T(8,128)S(1)}, u32[]{:S(2)}, u32[]{:S(2)}) async-start(f32[16,32,128]{2,1,0:T(8,128)} %copy-done.1), calls=%async_computation | async-start | bytes 524288 | tf_op jit(solution)/shard_map/all_to_all | solution.py:203
Sparse Core Ops, SparseCore 0:
  9.5 112.5 all-gather.4

commit v4 on v2

--- a/solution.py
+++ b/solution.py
@@ -9,16 +9,17 @@
 
 LANES = 128
 UNROLL = 32
-PIECES = 8
+PIECES = 16
 PAIRS = 4
+FINISH_BLOCKS = 4
 HIGHEST = lax.Precision.HIGHEST
 
 
 def gather_kernel(
     tile_ref, count_ref, pool_hbm, live_ref, weight_ref, noise_ref, draw_ref,
-    local_ref, edge_ref, pool, values, sems,
+    local_hbm, edge_ref, pool, values, local_ref, sems, local_sems,
 ):
-    blocks, cells, realizations = local_ref.shape
+    blocks, cells, _ = local_ref.shape
     halves, entries = values.shape[:2]
     edge = edge_ref.shape[1]
     rows = pool.shape[0] // PIECES
@@ -28,8 +29,8 @@
         )
         for i in range(PIECES)
     ]
-    for copy in copies:
-        copy.start()
+    for i, copy in enumerate(copies):
+        copy.start(priority=i % 2)
     values[...] = jnp.zeros_like(values)
     for b in range(blocks):
         local_ref[b] = jnp.dot(
@@ -37,6 +38,9 @@
         )
     for copy in copies:
         copy.wait()
+
+    def keep(b):
+        return pltpu.make_async_copy(local_ref.at[b], local_hbm.at[b], local_sems.at[b])
 
     def block(b, _):
         def some(i, _):
@@ -58,9 +62,12 @@
         local_ref[b] = total
         for h in range(halves):
             edge_ref[halves * b + h] = total[cells - edge :, h * LANES : (h + 1) * LANES]
+        keep(b).start()
         return 0
 
     lax.fori_loop(0, blocks, block, 0)
+    for b in range(blocks):
+        keep(b).wait()
 
 
 def gather_call(tile, count, pool, live, weight2, lower, draw, edge):
@@ -76,11 +83,13 @@
             jax.ShapeDtypeStruct((blocks * halves, edge, LANES), jnp.float32),
         ),
         in_specs=[smem, smem, pl.BlockSpec(memory_space=pl.ANY), vmem, vmem, vmem, vmem],
-        out_specs=(vmem, vmem),
+        out_specs=(pl.BlockSpec(memory_space=pl.ANY), vmem),
         scratch_shapes=[
             pltpu.VMEM(pool.shape, pool.dtype),
             pltpu.VMEM((halves, entries, 2, LANES), pool.dtype),
+            pltpu.VMEM((blocks, cells, realizations), jnp.float32),
             pltpu.SemaphoreType.DMA((PIECES,)),
+            pltpu.SemaphoreType.DMA((blocks,)),
         ],
         compiler_params=pltpu.CompilerParams(vmem_limit_bytes=50 * 2**20),
         cost_estimate=pl.CostEstimate(
@@ -108,27 +117,30 @@
 
 
 def finish_kernel(local_ref, face_ref, below_ref, out_ref):
-    halves = below_ref.shape[0]
-    below = jnp.concatenate([below_ref[h] for h in range(halves)], axis=1)
-    state = local_ref[0] + jnp.dot(
-        face_ref[...], below, precision=HIGHEST, preferred_element_type=jnp.float32
-    )
-    out_ref[0] = state.astype(out_ref.dtype)
+    blocks, _, realizations = local_ref.shape
+    halves = realizations // LANES
+    for b in range(blocks):
+        below = jnp.concatenate([below_ref[halves * b + h] for h in range(halves)], axis=1)
+        state = local_ref[b] + jnp.dot(
+            face_ref[...], below, precision=HIGHEST, preferred_element_type=jnp.float32
+        )
+        out_ref[b] = state.astype(out_ref.dtype)
 
 
 def finish_call(local, face, below):
     blocks, cells, realizations = local.shape
     edge = face.shape[1]
     halves = realizations // LANES
-    whole = pl.BlockSpec((1, cells, realizations), lambda b: (b, 0, 0))
+    size = FINISH_BLOCKS
+    whole = pl.BlockSpec((size, cells, realizations), lambda b: (b, 0, 0))
     return pl.pallas_call(
         finish_kernel,
-        grid=(blocks,),
+        grid=(blocks // size,),
         out_shape=jax.ShapeDtypeStruct(local.shape, jnp.bfloat16),
         in_specs=[
             whole,
             pl.BlockSpec((cells, edge), lambda b: (0, 0)),
-            pl.BlockSpec((halves, edge, LANES), lambda b: (b, 0, 0)),
+            pl.BlockSpec((size * halves, edge, LANES), lambda b: (b, 0, 0)),
         ],
         out_specs=whole,
         name="finish",

time: 186 us -> 183 us (0.984)
  Pallas kernels: 29.9 us -> 27.6 us
    pallas_call x1, Pallas kernels: 6.77 us -> 4.01 us  [finish_call(): pl.pallas_call(finish_kernel, grid=(blocks // size,), out_shape=jax.Shape...]
where the time goes in v4:
time: 183 us; the launch traced here: 182 us
  waiting for transfers between devices  108 us (59%)
  Pallas kernels  27.6 us (15%)
  between operations  13.6 us (7%)
  blocking collectives  10.9 us (6%)
  local copies, waits for them, and re-layouts  9.61 us (5%)
  starting transfers between devices  5.97 us (3%)
  other arithmetic  5.02 us (3%)
    all_gather x1, waiting for transfers between devices, body(): gathered = lax.all_gather(pool[0], 'tile', tiled=True)  99.7 us
    pallas_call x1, Pallas kernels, gather_call(): pl.pallas_call(gather_kernel, out_shape=(jax.ShapeDtypeStruct((blocks, ce...  22.6 us
    all_to_all x1, blocking collectives, body(): return finish_call(local, face_weight, swap(below))[None]  10.9 us
    all_to_all x1, waiting for transfers between devices, body(): below = scan_call(scan, swap(face).reshape(-1, LANES)).reshape(face.shape)  8.05 us
    all_to_all x1, starting transfers between devices, body(): below = scan_call(scan, swap(face).reshape(-1, LANES)).reshape(face.shape)  5.97 us
    pallas_call x1, Pallas kernels, finish_call(): pl.pallas_call(finish_kernel, grid=(blocks // size,), out_shape=jax.Shape...  4.01 us
    unnamed x25, local copies, waits for them, and re-layouts  3.69 us
  transfers between devices with their start and end apart: 2, of which 2 were waited for; matrix products, arithmetic and copies ran while one was open for 8% of the time, Pallas kernels for 0%

profile of v4, /device:TPU:1, one launch (start us, length us, event | category | flops | bytes accessed | tf_op | source)
XLA Modules:
  0.0 182.3 jit_solution(5026577943078189475)
XLA Ops:
  6.5 0.7 all-gather.3.cloned.1.call-update
  7.3 0.7 iota_compare_fusion
  8.0 0.5 and.48
  8.5 0.7 and.49
  9.2 1.2 copy.27
  10.3 0.8 fusion.27
  11.1 0.2 copy.24
  11.3 0.4 eq.37
  11.7 0.9 copy.25
  12.7 0.3 eq.40
  13.0 1.2 copy.28
  14.2 0.5 broadcast_in_dim.17
  14.8 0.4 reshape.109
  15.2 0.6 copy.29.weight_ref
  15.9 0.9 copy.31.face_ref
  16.9 0.2 fusion.32
  17.1 0.1 fusion.48
  17.2 0.2 fusion.36
  17.5 0.1 fusion.49
  17.6 0.3 fusion.19
  18.8 0.8 fusion.31
  19.6 0.8 fusion.17.tile_ref
  20.4 0.9 fusion.noise_ref
  21.3 0.9 and_convert_fusion.live_ref
  22.3 99.7 %all-gather.3.cloned.1.call-done = bf16[1,32768,256]{2,1,0:T(8,128)(2,1)} async-done(((bf16[1,1024,256]{2,1,0:T(8,128)(2,1)}), bf16[1,32768,256]{2,1,0:T(8,128)(2,1)}) %all-gather.3.cloned.1.call-update) | async-done | bytes 16777232 | tf_op jit(solution)/shard_map/all_gather | solution.py:173
  122.0 22.6 %gather.1 = (f32[8,256,256]{2,1,0:T(8,128)}, f32[16,32,128]{2,1,0:T(8,128)S(1)}) custom-call(s32[8192]{0:T(1024)S(1)} %fusion.17.tile_ref, s32[8]{0:T(128)S(1)} %bitcast.44, bf16[32768,2,128]{2,1,0:T(2,128)(2,1)} %bitcast.45, bf16[8,1,2048]{2,1,0:T(2,128)(2,1)S(1)} %and_convert_fusion.live_ref, bf16[256,2048]{1,0:T(8,128)(2,1)S(1)} %copy.29.weight_ref, ...), custom_call_target="tpu_custom_call" | custom-call | flops 2415919104 | bytes 83886080 | tf_op jit(solution)/shard_map/gather/pallas_call | solution.py:79
  144.6 0.7 copy-done.1
  145.3 6.0 %all-to-all-start = ((f32[16,32,128]{2,1,0:T(8,128)}), f32[16,32,128]{2,1,0:T(8,128)S(1)}, u32[]{:S(2)}, u32[]{:S(2)}) async-start(f32[16,32,128]{2,1,0:T(8,128)} %copy-done.1), calls=%async_computation | async-start | bytes 524288 | tf_op jit(solution)/shard_map/all_to_all | solution.py:190
  151.5 8.1 %all-to-all-done = f32[16,32,128]{2,1,0:T(8,128)S(1)} async-done(((f32[16,32,128]{2,1,0:T(8,128)}), f32[16,32,128]{2,1,0:T(8,128)S(1)}, u32[]{:S(2)}, u32[]{:S(2)}) %all-to-all-start) | async-done | bytes 262176 | tf_op jit(solution)/shard_map/all_to_all | solution.py:190
  159.5 1.0 scan.1
  160.6 10.9 %all_to_all.10.below_ref = f32[16,32,128]{2,1,0:T(8,128)} all-to-all(f32[16,32,128]{2,1,0:T(8,128)S(1)} %bitcast.42), channel_id=1, replica_groups=mesh['front'=16,'tile'=32] {'front'}, dimensions={0} | all-to-all | bytes 524288 | tf_op jit(solution)/shard_map/all_to_all | solution.py:191
  171.5 4.0 %finish.1 = bf16[8,256,256]{2,1,0:T(8,128)(2,1)} custom-call(f32[8,256,256]{2,1,0:T(8,128)} %get-tuple-element.7.local_ref, f32[256,32]{1,0:T(8,128)} %copy-done.3, f32[16,32,128]{2,1,0:T(8,128)} %all_to_all.10.below_ref), custom_call_target="tpu_custom_call" | custom-call | tf_op jit(solution)/shard_map/finish/pallas_call | solution.py:136
  (30 shorter events, 1.3 us)
Async XLA Ops:
  6.5 115.5 %copy-start.2 = (s32[1,8]{1,0:T(1,128)S(1)}, s32[1,8]{1,0:T(1,128)}, u32[]{:S(2)}) copy-start(s32[1,8]{1,0:T(1,128)} %param.11) | copy-start | bytes 100
  6.5 115.5 %copy-start = (bf16[1,8,256,256]{3,2,1,0:T(8,128)(2,1)S(1)}, bf16[1,8,256,256]{3,2,1,0:T(8,128)(2,1)}, u32[]{:S(2)}) copy-start(bf16[1,8,256,256]{3,2,1,0:T(8,128)(2,1)} %param.12) | copy-start | bytes 3145732
  6.5 115.5 %all-gather.3.cloned.1.call-start = ((), (), s32[]{:S(2)}) async-start(), calls=%async_computation.2 | async-start | bytes 17301504 | tf_op jit(solution)/shard_map/all_gather | solution.py:173
  16.7 1.3 copy-start.3
  144.6 0.7 copy-start.1
  145.3 14.2 %all-to-all-start = ((f32[16,32,128]{2,1,0:T(8,128)}), f32[16,32,128]{2,1,0:T(8,128)S(1)}, u32[]{:S(2)}, u32[]{:S(2)}) async-start(f32[16,32,128]{2,1,0:T(8,128)} %copy-done.1), calls=%async_computation | async-start | bytes 524288 | tf_op jit(solution)/shard_map/all_to_all | solution.py:190
Sparse Core Ops, SparseCore 0:
  9.5 112.4 all-gather.2

commit v5 on v4

--- a/solution.py
+++ b/solution.py
@@ -11,13 +11,12 @@
 UNROLL = 32
 PIECES = 16
 PAIRS = 4
-FINISH_BLOCKS = 4
 HIGHEST = lax.Precision.HIGHEST
 
 
 def gather_kernel(
     tile_ref, count_ref, pool_hbm, live_ref, weight_ref, noise_ref, draw_ref,
-    local_hbm, edge_ref, pool, values, local_ref, sems, local_sems,
+    local_ref, edge_ref, pool, values, sems,
 ):
     blocks, cells, _ = local_ref.shape
     halves, entries = values.shape[:2]
@@ -29,8 +28,8 @@
         )
         for i in range(PIECES)
     ]
-    for i, copy in enumerate(copies):
-        copy.start(priority=i % 2)
+    for copy in copies:
+        copy.start()
     values[...] = jnp.zeros_like(values)
     for b in range(blocks):
         local_ref[b] = jnp.dot(
@@ -38,9 +37,6 @@
         )
     for copy in copies:
         copy.wait()
-
-    def keep(b):
-        return pltpu.make_async_copy(local_ref.at[b], local_hbm.at[b], local_sems.at[b])
 
     def block(b, _):
         def some(i, _):
@@ -62,12 +58,9 @@
         local_ref[b] = total
         for h in range(halves):
             edge_ref[halves * b + h] = total[cells - edge :, h * LANES : (h + 1) * LANES]
-        keep(b).start()
         return 0
 
     lax.fori_loop(0, blocks, block, 0)
-    for b in range(blocks):
-        keep(b).wait()
 
 
 def gather_call(tile, count, pool, live, weight2, lower, draw, edge):
@@ -82,16 +75,14 @@
             jax.ShapeDtypeStruct((blocks, cells, realizations), jnp.float32),
             jax.ShapeDtypeStruct((blocks * halves, edge, LANES), jnp.float32),
         ),
-        in_specs=[smem, smem, pl.BlockSpec(memory_space=pl.ANY), vmem, vmem, vmem, vmem],
-        out_specs=(pl.BlockSpec(memory_space=pl.ANY), vmem),
+        in_specs=[smem, smem, pl.BlockSpec(memory_space=pltpu.HBM), vmem, vmem, vmem, vmem],
+        out_specs=(vmem, vmem),
         scratch_shapes=[
             pltpu.VMEM(pool.shape, pool.dtype),
             pltpu.VMEM((halves, entries, 2, LANES), pool.dtype),
-            pltpu.VMEM((blocks, cells, realizations), jnp.float32),
             pltpu.SemaphoreType.DMA((PIECES,)),
-            pltpu.SemaphoreType.DMA((blocks,)),
         ],
-        compiler_params=pltpu.CompilerParams(vmem_limit_bytes=50 * 2**20),
+        compiler_params=pltpu.CompilerParams(vmem_limit_bytes=46 * 2**20),
         cost_estimate=pl.CostEstimate(
             flops=2 * blocks * cells * (2 * entries + cells) * realizations,
             bytes_accessed=5 * 2**24,
@@ -128,21 +119,10 @@
 
 
 def finish_call(local, face, below):
-    blocks, cells, realizations = local.shape
-    edge = face.shape[1]
-    halves = realizations // LANES
-    size = FINISH_BLOCKS
-    whole = pl.BlockSpec((size, cells, realizations), lambda b: (b, 0, 0))
     return pl.pallas_call(
         finish_kernel,
-        grid=(blocks // size,),
         out_shape=jax.ShapeDtypeStruct(local.shape, jnp.bfloat16),
-        in_specs=[
-            whole,
-            pl.BlockSpec((cells, edge), lambda b: (0, 0)),
-            pl.BlockSpec((size * halves, edge, LANES), lambda b: (b, 0, 0)),
-        ],
-        out_specs=whole,
+        compiler_params=pltpu.CompilerParams(vmem_limit_bytes=12 * 2**20),
         name="finish",
     )(local, face, below)
 

time: 183 us -> 183 us (level)
  local copies, waits for them, and re-layouts: 9.61 us -> 22.8 us
  waiting for transfers between devices: 108 us -> 96.8 us
  Pallas kernels: 27.6 us -> 25.3 us
    unnamed x25, local copies, waits for them, and re-layouts: 3.69 us -> 16.1 us
    all_gather x1, waiting for transfers between devices: 99.7 us -> 93 us  [body(): gathered = lax.all_gather(pool[0], 'tile', tiled=True)]
    all_to_all x1, waiting for transfers between devices: 8.05 us -> 3.11 us  [body(): below = scan_call(scan, swap(face).reshape(-1, LANES)).reshape(face.shape)]
    pallas_call x1, Pallas kernels: 22.6 us -> 20.3 us  [gather_call(): pl.pallas_call(gather_kernel, out_shape=(jax.ShapeDtypeStruct((blocks, ce...]
  transfers between devices with their start and end apart: 2 -> 2, of which waited for: 2 -> 2; matrix products, arithmetic and copies ran while one was open for 8% -> 14% of each run, Pallas kernels for 0% -> 0%
where the time goes in v5:
time: 183 us; the launch traced here: 181 us
  waiting for transfers between devices  96.8 us (53%)
  Pallas kernels  25.3 us (14%)
  local copies, waits for them, and re-layouts  22.8 us (12%)
  between operations  13.6 us (7%)
  blocking collectives  11 us (6%)
  starting transfers between devices  6.43 us (4%)
  other arithmetic  4.17 us (2%)
    all_gather x1, waiting for transfers between devices, body(): gathered = lax.all_gather(pool[0], 'tile', tiled=True)  93 us
    pallas_call x1, Pallas kernels, gather_call(): pl.pallas_call(gather_kernel, out_shape=(jax.ShapeDtypeStruct((blocks, ce...  20.3 us
    unnamed x25, local copies, waits for them, and re-layouts  16.1 us
    all_to_all x1, blocking collectives, body(): return finish_call(local, face_weight, swap(below))[None]  11 us
    all_to_all x1, starting transfers between devices, body(): below = scan_call(scan, swap(face).reshape(-1, LANES)).reshape(face.shape)  6.43 us
  transfers between devices with their start and end apart: 2, of which 2 were waited for; matrix products, arithmetic and copies ran while one was open for 14% of the time, Pallas kernels for 0%

profile of v5, /device:TPU:1, one launch (start us, length us, event | category | flops | bytes accessed | tf_op | source)
XLA Modules:
  0.0 181.2 jit_solution(15036664505645002033)
XLA Ops:
  6.5 0.7 all-gather.3.cloned.1.call-update
  7.3 0.7 iota_compare_fusion
  8.5 0.7 and.49
  9.2 1.2 copy.27
  10.3 0.8 fusion.27
  12.3 1.2 copy.28
  15.2 0.9 copy.31.face_ref
  17.4 0.7 constant_dynamic-update-slice_fusion
  18.1 0.7 fusion.1
  18.8 0.7 fusion.2
  20.1 0.7 fusion.4
  20.8 0.7 fusion.5
  21.5 0.7 fusion.6
  22.9 0.7 fusion.8
  23.6 0.7 fusion.9
  24.3 0.7 fusion.10
  25.6 0.7 fusion.12
  26.3 0.8 fusion.31
  27.1 0.8 fusion.17.tile_ref
  28.0 0.9 fusion.noise_ref
  29.0 93.0 %all-gather.3.cloned.1.call-done = bf16[1,32768,256]{2,1,0:T(8,128)(2,1)} async-done(((bf16[1,1024,256]{2,1,0:T(8,128)(2,1)}), bf16[1,32768,256]{2,1,0:T(8,128)(2,1)}) %all-gather.3.cloned.1.call-update) | async-done | bytes 16777232 | tf_op jit(solution)/shard_map/all_gather | solution.py:153
  122.0 1.2 copy-done
  123.2 20.3 %gather.1 = (f32[8,256,256]{2,1,0:T(8,128)S(1)}, f32[16,32,128]{2,1,0:T(8,128)S(1)}) custom-call(s32[8192]{0:T(1024)S(1)} %fusion.17.tile_ref, s32[8]{0:T(128)S(1)} %bitcast.44, bf16[32768,2,128]{2,1,0:T(2,128)(2,1)} %bitcast.45, bf16[8,1,2048]{2,1,0:T(2,128)(2,1)S(1)} %and_convert_fusion.live_ref, bf16[256,2048]{1,0:T(8,128)(2,1)S(1)} %copy.29.weight_ref, ...), custom_call_target="tpu_custom_call" | custom-call | flops 2415919104 | bytes 83886080 | tf_op jit(solution)/shard_map/gather/pallas_call | solution.py:72
  143.6 0.7 copy-done.1
  144.3 6.4 %all-to-all-start = ((f32[16,32,128]{2,1,0:T(8,128)}), f32[16,32,128]{2,1,0:T(8,128)S(1)}, u32[]{:S(2)}, u32[]{:S(2)}) async-start(f32[16,32,128]{2,1,0:T(8,128)} %copy-done.1), calls=%async_computation | async-start | bytes 524288 | tf_op jit(solution)/shard_map/all_to_all | solution.py:170
  150.7 1.6 fusion.13
  152.3 1.6 fusion.14
  153.8 1.5 fusion.15.scan_ref
  155.3 3.1 %all-to-all-done = f32[16,32,128]{2,1,0:T(8,128)S(1)} async-done(((f32[16,32,128]{2,1,0:T(8,128)}), f32[16,32,128]{2,1,0:T(8,128)S(1)}, u32[]{:S(2)}, u32[]{:S(2)}) %all-to-all-start) | async-done | bytes 262176 | tf_op jit(solution)/shard_map/all_to_all | solution.py:170
  158.4 2.2 %scan.1 = f32[512,128]{1,0:T(8,128)S(1)} custom-call(f32[512,512]{1,0:T(8,128)} %fusion.15.scan_ref, f32[512,128]{1,0:T(8,128)S(1)} %bitcast.41), custom_call_target="tpu_custom_call" | custom-call | tf_op jit(solution)/shard_map/scan/pallas_call | solution.py:102
  160.7 11.0 %all_to_all.10.below_ref = f32[16,32,128]{2,1,0:T(8,128)S(1)} all-to-all(f32[16,32,128]{2,1,0:T(8,128)S(1)} %bitcast.42), channel_id=1, replica_groups=mesh['front'=16,'tile'=32] {'front'}, dimensions={0} | all-to-all | bytes 524288 | tf_op jit(solution)/shard_map/all_to_all | solution.py:171
  171.6 2.7 %finish.1 = bf16[8,256,256]{2,1,0:T(8,128)(2,1)} custom-call(f32[8,256,256]{2,1,0:T(8,128)S(1)} %get-tuple-element.7.local_ref, f32[256,32]{1,0:T(8,128)S(1)} %copy.31.face_ref, f32[16,32,128]{2,1,0:T(8,128)S(1)} %all_to_all.10.below_ref), custom_call_target="tpu_custom_call" | custom-call | tf_op jit(solution)/shard_map/finish/pallas_call | solution.py:122
  (30 shorter events, 6.6 us)
Async XLA Ops:
  6.5 115.5 %copy-start.2 = (s32[1,8]{1,0:T(1,128)S(1)}, s32[1,8]{1,0:T(1,128)}, u32[]{:S(2)}) copy-start(s32[1,8]{1,0:T(1,128)} %param.11) | copy-start | bytes 100
  6.5 115.5 %all-gather.3.cloned.1.call-start = ((), (), s32[]{:S(2)}) async-start(), calls=%async_computation.2 | async-start | bytes 17301504 | tf_op jit(solution)/shard_map/all_gather | solution.py:153
  17.4 10.5 %copy-start.3 = (f32[32,480]{1,0:T(8,128)}, f32[32,480]{1,0:T(8,128)S(1)}, u32[]{:S(2)}) copy-start(f32[32,480]{1,0:T(8,128)S(1)} %slice.69) | copy-start | bytes 184324
  122.0 1.2 copy-start
  143.6 0.7 copy-start.1
  144.3 14.1 %all-to-all-start = ((f32[16,32,128]{2,1,0:T(8,128)}), f32[16,32,128]{2,1,0:T(8,128)S(1)}, u32[]{:S(2)}, u32[]{:S(2)}) async-start(f32[16,32,128]{2,1,0:T(8,128)} %copy-done.1), calls=%async_computation | async-start | bytes 524288 | tf_op jit(solution)/shard_map/all_to_all | solution.py:170
Sparse Core Ops, SparseCore 0:
  9.5 112.4 all-gather.2

commit v6 on v5

--- a/solution.py
+++ b/solution.py
@@ -92,43 +92,57 @@
     )(tile, count, pool, live, weight2, lower, draw)
 
 
-def scan_kernel(scan_ref, face_ref, out_ref):
-    out_ref[...] = jnp.dot(
-        scan_ref[...], face_ref[...], precision=HIGHEST, preferred_element_type=jnp.float32
-    )
-
-
-def scan_call(scan, face):
+def scan_kernel(near_ref, far_ref, face_ref, out_ref):
+    mm = functools.partial(jnp.dot, precision=HIGHEST, preferred_element_type=jnp.float32)
+    half = near_ref.shape[0]
+    low, high = face_ref[:half], face_ref[half:]
+    out_ref[:half] = mm(near_ref[...], low)
+    out_ref[half:] = mm(far_ref[...], low) + mm(near_ref[...], high)
+
+
+def scan_call(near, far, face):
     return pl.pallas_call(
         scan_kernel,
         out_shape=jax.ShapeDtypeStruct(face.shape, face.dtype),
-        compiler_params=pltpu.CompilerParams(vmem_limit_bytes=16 * 2**20),
+        compiler_params=pltpu.CompilerParams(vmem_limit_bytes=12 * 2**20),
         name="scan",
-    )(scan, face)
-
-
-def finish_kernel(local_ref, face_ref, below_ref, out_ref):
+    )(near, far, face)
+
+
+def finish_kernel(local_ref, face_ref, below_ref, out_hbm, done, sems):
     blocks, _, realizations = local_ref.shape
     halves = realizations // LANES
+    copies = [pltpu.make_async_copy(done.at[b], out_hbm.at[b], sems.at[b]) for b in range(blocks)]
     for b in range(blocks):
         below = jnp.concatenate([below_ref[halves * b + h] for h in range(halves)], axis=1)
         state = local_ref[b] + jnp.dot(
             face_ref[...], below, precision=HIGHEST, preferred_element_type=jnp.float32
         )
-        out_ref[b] = state.astype(out_ref.dtype)
+        done[b] = state.astype(done.dtype)
+        copies[b].start()
+    for copy in copies:
+        copy.wait()
 
 
 def finish_call(local, face, below):
+    vmem = pl.BlockSpec(memory_space=pltpu.VMEM)
     return pl.pallas_call(
         finish_kernel,
         out_shape=jax.ShapeDtypeStruct(local.shape, jnp.bfloat16),
+        in_specs=[vmem, vmem, vmem],
+        out_specs=pl.BlockSpec(memory_space=pl.ANY),
+        scratch_shapes=[
+            pltpu.VMEM(local.shape, jnp.bfloat16),
+            pltpu.SemaphoreType.DMA((local.shape[0],)),
+        ],
         compiler_params=pltpu.CompilerParams(vmem_limit_bytes=12 * 2**20),
         name="finish",
     )(local, face, below)
 
 
-def scan_matrix(square, count):
+def scan_matrices(square, count):
     edge = square.shape[0]
+    half = count // 2
     mm = functools.partial(jnp.dot, precision=HIGHEST)
     powers = jnp.concatenate([square, jnp.eye(edge, dtype=square.dtype)], axis=1)
     top = mm(square, square)
@@ -136,9 +150,13 @@
         powers = jnp.concatenate([mm(top, powers), powers], axis=1)
         top = mm(top, top)
     powers = powers[:, -(count - 1) * edge :]
-    strip = jnp.concatenate([powers, jnp.zeros((edge, count * edge), powers.dtype)], axis=1)
-    starts = [(count - 1 - f) * edge for f in range(count)]
-    return jnp.concatenate([strip[:, s : s + count * edge] for s in starts])
+    strip = jnp.concatenate([powers, jnp.zeros((edge, half * edge), powers.dtype)], axis=1)
+
+    def rows(first):
+        starts = [(count - 1 - first - f) * edge for f in range(half)]
+        return jnp.concatenate([strip[:, s : s + half * edge] for s in starts])
+
+    return rows(0), rows(half)
 
 
 def body(
@@ -160,14 +178,14 @@
     live = (index & 1)[:, :, None] == jnp.arange(2)[None, None, :]
     live = (live & is_live[:, :, None]).astype(jnp.bfloat16).reshape(-1, 1, 2 * entries)
     weight2 = jnp.repeat(kriging_weight, 2, axis=1)
-    scan = scan_matrix(face_weight[-edge:], front_count)
+    near, far = scan_matrices(face_weight[-edge:], front_count)
     local, face = gather_call(
         tile.reshape(-1), count, pieces, live, weight2, jnp.tril(noise_factor), normal_draw[0], edge
     )
     swap = functools.partial(
         lax.all_to_all, axis_name="front", split_axis=0, concat_axis=0, tiled=True
     )
-    below = scan_call(scan, swap(face).reshape(-1, LANES)).reshape(face.shape)
+    below = scan_call(near, far, swap(face).reshape(-1, LANES)).reshape(face.shape)
     return finish_call(local, face_weight, swap(below))[None]
 
 

time: 183 us -> 183 us (level)
  local copies, waits for them, and re-layouts: 22.8 us -> 12.4 us
  waiting for transfers between devices: 96.8 us -> 107 us
  other arithmetic: 4.17 us -> 7.18 us
  Pallas kernels: 25.3 us -> 23.4 us
    unnamed x25 -> x27, local copies, waits for them, and re-layouts: 16.1 us -> 7.12 us
    all_gather x1, waiting for transfers between devices: 93 us -> 101 us  [body(): gathered = lax.all_gather(pool[0], 'tile', tiled=True)]
    all_to_all x1, waiting for transfers between devices: 3.11 us -> 5.2 us  [body(): swap(face).reshape(-1, LANES)]
  transfers between devices with their start and end apart: 2 -> 2, of which waited for: 2 -> 2; matrix products, arithmetic and copies ran while one was open for 14% -> 9% of each run, Pallas kernels for 0% -> 0%
where the time goes in v6:
time: 183 us; the launch traced here: 182 us
  waiting for transfers between devices  107 us (58%)
  Pallas kernels  23.4 us (13%)
  between operations  13.6 us (7%)
  local copies, waits for them, and re-layouts  12.4 us (7%)
  blocking collectives  10.2 us (6%)
  other arithmetic  7.18 us (4%)
  starting transfers between devices  7.11 us (4%)
    all_gather x1, waiting for transfers between devices, body(): gathered = lax.all_gather(pool[0], 'tile', tiled=True)  101 us
    pallas_call x1, Pallas kernels, gather_call(): pl.pallas_call(gather_kernel, out_shape=(jax.ShapeDtypeStruct((blocks, ce...  20 us
    all_to_all x1, blocking collectives, body(): return finish_call(local, face_weight, swap(below))[None]  10.2 us
    unnamed x27, local copies, waits for them, and re-layouts  7.12 us
    all_to_all x1, starting transfers between devices, body(): swap(face).reshape(-1, LANES)  7.11 us
    all_to_all x1, waiting for transfers between devices, body(): swap(face).reshape(-1, LANES)  5.2 us
  transfers between devices with their start and end apart: 2, of which 2 were waited for; matrix products, arithmetic and copies ran while one was open for 9% of the time, Pallas kernels for 0%

profile of v6, /device:TPU:1, one launch (start us, length us, event | category | flops | bytes accessed | tf_op | source)
XLA Modules:
  0.0 182.0 jit_solution(916381041421132765)
XLA Ops:
  6.5 0.7 all-gather.3.cloned.1.call-update
  7.3 0.7 iota_compare_fusion
  8.0 0.5 and.48
  8.5 0.7 and.49
  9.2 1.2 copy.27
  10.3 0.8 fusion.7
  11.3 0.4 eq.37
  11.7 0.3 copy.25
  12.1 0.3 eq.40
  12.3 1.2 copy.28
  13.6 0.5 broadcast_in_dim.17
  14.1 0.4 reshape.109
  14.6 0.6 copy.29.weight_ref
  15.2 0.9 copy.31.face_ref
  18.2 0.8 fusion.11
  18.9 0.8 fusion.2.tile_ref
  19.8 0.9 fusion.noise_ref
  20.8 101.2 %all-gather.3.cloned.1.call-done = bf16[1,32768,256]{2,1,0:T(8,128)(2,1)} async-done(((bf16[1,1024,256]{2,1,0:T(8,128)(2,1)}), bf16[1,32768,256]{2,1,0:T(8,128)(2,1)}) %all-gather.3.cloned.1.call-update) | async-done | bytes 16777232 | tf_op jit(solution)/shard_map/all_gather | solution.py:171
  122.0 1.2 copy-done
  123.2 0.7 copy-done.6
  123.9 20.0 %gather.1 = (f32[8,256,256]{2,1,0:T(8,128)S(1)}, f32[16,32,128]{2,1,0:T(8,128)S(1)}) custom-call(s32[8192]{0:T(1024)S(1)} %fusion.2.tile_ref, s32[8]{0:T(128)S(1)} %bitcast.44, bf16[32768,2,128]{2,1,0:T(2,128)(2,1)} %bitcast.45, bf16[8,1,2048]{2,1,0:T(2,128)(2,1)S(1)} %and_convert_fusion.live_ref, bf16[256,2048]{1,0:T(8,128)(2,1)S(1)} %copy.29.weight_ref, ...), custom_call_target="tpu_custom_call" | custom-call | flops 2415919104 | bytes 83886080 | tf_op jit(solution)/shard_map/gather/pallas_call | solution.py:72
  144.0 0.7 copy-done.5
  144.7 7.1 %all-to-all-start = ((f32[16,32,128]{2,1,0:T(8,128)}), f32[16,32,128]{2,1,0:T(8,128)S(1)}, u32[]{:S(2)}, u32[]{:S(2)}) async-start(f32[16,32,128]{2,1,0:T(8,128)} %copy-done.5), calls=%async_computation | async-start | bytes 524288 | tf_op jit(solution)/shard_map/all_to_all | solution.py:188
  151.8 0.7 constant_dynamic-update-slice_fusion.10
  152.5 0.7 constant_dynamic-update-slice_fusion.9
  153.2 1.4 constant_dynamic-update-slice_fusion
  154.6 5.2 %all-to-all-done = f32[16,32,128]{2,1,0:T(8,128)S(1)} async-done(((f32[16,32,128]{2,1,0:T(8,128)}), f32[16,32,128]{2,1,0:T(8,128)S(1)}, u32[]{:S(2)}, u32[]{:S(2)}) %all-to-all-start) | async-done | bytes 262176 | tf_op jit(solution)/shard_map/all_to_all | solution.py:188
  159.8 0.9 copy-done.2
  160.8 0.9 copy-done.4
  161.7 0.8 scan.1
  162.5 10.2 %all_to_all.10.below_ref = f32[16,32,128]{2,1,0:T(8,128)S(1)} all-to-all(f32[16,32,128]{2,1,0:T(8,128)S(1)} %bitcast.42), channel_id=1, replica_groups=mesh['front'=16,'tile'=32] {'front'}, dimensions={0} | all-to-all | bytes 524288 | tf_op jit(solution)/shard_map/all_to_all | solution.py:189
  172.6 2.5 %finish.1 = bf16[8,256,256]{2,1,0:T(8,128)(2,1)} custom-call(f32[8,256,256]{2,1,0:T(8,128)S(1)} %get-tuple-element.7.local_ref, f32[256,32]{1,0:T(8,128)S(1)} %copy.31.face_ref, f32[16,32,128]{2,1,0:T(8,128)S(1)} %all_to_all.10.below_ref), custom_call_target="tpu_custom_call" | custom-call | tf_op jit(solution)/shard_map/finish/pallas_call | solution.py:129
  (38 shorter events, 2.4 us)
Async XLA Ops:
  6.5 115.5 %all-gather.3.cloned.1.call-start = ((), (), s32[]{:S(2)}) async-start(), calls=%async_computation.2 | async-start | bytes 17301504 | tf_op jit(solution)/shard_map/all_gather | solution.py:171
  17.4 3.3 %copy-start.7 = (f32[32,480]{1,0:T(8,128)}, f32[32,480]{1,0:T(8,128)S(1)}, u32[]{:S(2)}) copy-start(f32[32,480]{1,0:T(8,128)S(1)} %slice.82) | copy-start | bytes 184324
  17.9 1.9 %copy-start.3 = (f32[256,256]{1,0:T(8,128)}, f32[256,256]{1,0:T(8,128)S(1)}, u32[]{:S(2)}) copy-start(f32[256,256]{1,0:T(8,128)S(1)} %constant_dynamic-update-slice_fusion.1) | copy-start | bytes 786436
  18.2 0.8 copy-start.1
  122.0 1.2 copy-start
  123.2 0.7 copy-start.6
  143.9 0.7 copy-start.5
  144.7 15.1 %all-to-all-start = ((f32[16,32,128]{2,1,0:T(8,128)}), f32[16,32,128]{2,1,0:T(8,128)S(1)}, u32[]{:S(2)}, u32[]{:S(2)}) async-start(f32[16,32,128]{2,1,0:T(8,128)} %copy-done.5), calls=%async_computation | async-start | bytes 524288 | tf_op jit(solution)/shard_map/all_to_all | solution.py:188
  159.8 1.0 copy-start.2
  160.8 0.9 copy-start.4
Sparse Core Ops, SparseCore 0:
  9.5 112.4 all-gather.2

commit v7 on v6

--- a/solution.py
+++ b/solution.py
@@ -92,21 +92,28 @@
     )(tile, count, pool, live, weight2, lower, draw)
 
 
-def scan_kernel(near_ref, far_ref, face_ref, out_ref):
+def scan_kernel(strip_ref, face_ref, out_ref, near, far):
     mm = functools.partial(jnp.dot, precision=HIGHEST, preferred_element_type=jnp.float32)
-    half = near_ref.shape[0]
+    edge, half = strip_ref.shape[0], near.shape[0]
+    fronts = 2 * half // edge
+    for f in range(fronts // 2):
+        for matrix, first in ((near, 0), (far, fronts // 2)):
+            start = (fronts - 1 - first - f) * edge
+            matrix[f * edge : (f + 1) * edge, :] = strip_ref[:, start : start + half]
     low, high = face_ref[:half], face_ref[half:]
-    out_ref[:half] = mm(near_ref[...], low)
-    out_ref[half:] = mm(far_ref[...], low) + mm(near_ref[...], high)
-
-
-def scan_call(near, far, face):
+    out_ref[:half] = mm(near[...], low)
+    out_ref[half:] = mm(far[...], low) + mm(near[...], high)
+
+
+def scan_call(strip, face):
+    half = face.shape[0] // 2
     return pl.pallas_call(
         scan_kernel,
         out_shape=jax.ShapeDtypeStruct(face.shape, face.dtype),
+        scratch_shapes=[pltpu.VMEM((half, half), face.dtype)] * 2,
         compiler_params=pltpu.CompilerParams(vmem_limit_bytes=12 * 2**20),
         name="scan",
-    )(near, far, face)
+    )(strip, face)
 
 
 def finish_kernel(local_ref, face_ref, below_ref, out_hbm, done, sems):
@@ -140,9 +147,8 @@
     )(local, face, below)
 
 
-def scan_matrices(square, count):
+def scan_strip(square, count):
     edge = square.shape[0]
-    half = count // 2
     mm = functools.partial(jnp.dot, precision=HIGHEST)
     powers = jnp.concatenate([square, jnp.eye(edge, dtype=square.dtype)], axis=1)
     top = mm(square, square)
@@ -150,13 +156,8 @@
         powers = jnp.concatenate([mm(top, powers), powers], axis=1)
         top = mm(top, top)
     powers = powers[:, -(count - 1) * edge :]
-    strip = jnp.concatenate([powers, jnp.zeros((edge, half * edge), powers.dtype)], axis=1)
-
-    def rows(first):
-        starts = [(count - 1 - first - f) * edge for f in range(half)]
-        return jnp.concatenate([strip[:, s : s + half * edge] for s in starts])
-
-    return rows(0), rows(half)
+    zeros = jnp.zeros((edge, count // 2 * edge), powers.dtype)
+    return jnp.concatenate([powers, zeros], axis=1)
 
 
 def body(
@@ -178,14 +179,14 @@
     live = (index & 1)[:, :, None] == jnp.arange(2)[None, None, :]
     live = (live & is_live[:, :, None]).astype(jnp.bfloat16).reshape(-1, 1, 2 * entries)
     weight2 = jnp.repeat(kriging_weight, 2, axis=1)
-    near, far = scan_matrices(face_weight[-edge:], front_count)
+    strip = scan_strip(face_weight[-edge:], front_count)
     local, face = gather_call(
         tile.reshape(-1), count, pieces, live, weight2, jnp.tril(noise_factor), normal_draw[0], edge
     )
     swap = functools.partial(
         lax.all_to_all, axis_name="front", split_axis=0, concat_axis=0, tiled=True
     )
-    below = scan_call(near, far, swap(face).reshape(-1, LANES)).reshape(face.shape)
+    below = scan_call(strip, swap(face).reshape(-1, LANES)).reshape(face.shape)
     return finish_call(local, face_weight, swap(below))[None]
 
 

time: 183 us -> 182 us (level)
  other arithmetic: 7.18 us -> 4.87 us
  matrix products: 1.11 us -> 3.12 us
    unnamed x27 -> x10, local copies, waits for them, and re-layouts: 7.12 us -> 4.69 us
    dot_general x6, matrix products: 1.11 us -> 3.12 us  [the longest x3 2.11 us: scan_strip(): powers = jnp.concatenate([mm(top, powers), powers], axis=1)]
where the time goes in v7:
time: 182 us; the launch traced here: 181 us
  waiting for transfers between devices  108 us (59%)
  Pallas kernels  24.2 us (13%)
  between operations  13.6 us (7%)
  local copies, waits for them, and re-layouts  10.6 us (6%)
  blocking collectives  10.2 us (6%)
  starting transfers between devices  6.39 us (4%)
  other arithmetic  4.87 us (3%)
  matrix products  3.12 us (2%)
    all_gather x1, waiting for transfers between devices, body(): gathered = lax.all_gather(pool[0], 'tile', tiled=True)  101 us
    pallas_call x1, Pallas kernels, gather_call(): pl.pallas_call(gather_kernel, out_shape=(jax.ShapeDtypeStruct((blocks, ce...  20.8 us
    all_to_all x1, blocking collectives, body(): return finish_call(local, face_weight, swap(below))[None]  10.2 us
    all_to_all x1, starting transfers between devices, body(): below = scan_call(strip, swap(face).reshape(-1, LANES)).reshape(face.shape)  6.39 us
    all_to_all x1, waiting for transfers between devices, body(): below = scan_call(strip, swap(face).reshape(-1, LANES)).reshape(face.shape)  6.3 us
    unnamed x10, local copies, waits for them, and re-layouts  4.69 us
  transfers between devices with their start and end apart: 2, of which 2 were waited for; matrix products, arithmetic and copies ran while one was open for 9% of the time, Pallas kernels for 0%

profile of v7, /device:TPU:1, one launch (start us, length us, event | category | flops | bytes accessed | tf_op | source)
XLA Modules:
  0.0 180.7 jit_solution(17505929143449007727)
XLA Ops:
  6.5 0.7 all-gather.3.cloned.1.call-update
  7.3 0.7 iota_compare_fusion
  8.0 0.5 and.48
  8.5 0.7 and.49
  9.2 1.2 copy.27
  10.3 0.8 fusion.12
  11.3 0.4 eq.37
  11.7 0.3 copy.25
  12.1 0.9 eq.40
  12.9 1.2 copy.28
  14.2 0.5 broadcast_in_dim.8
  14.7 0.4 reshape.109
  15.2 0.6 copy.29.weight_ref
  15.8 0.9 copy.31.face_ref
  16.8 0.2 fusion.17
  17.2 0.7 fusion.34
  18.0 0.8 fusion.16
  18.7 0.8 fusion.2.tile_ref
  19.6 0.9 fusion.noise_ref
  20.5 0.8 and_convert_fusion.live_ref
  21.3 100.7 %all-gather.3.cloned.1.call-done = bf16[1,32768,256]{2,1,0:T(8,128)(2,1)} async-done(((bf16[1,1024,256]{2,1,0:T(8,128)(2,1)}), bf16[1,32768,256]{2,1,0:T(8,128)(2,1)}) %all-gather.3.cloned.1.call-update) | async-done | bytes 16777232 | tf_op jit(solution)/shard_map/all_gather | solution.py:172
  122.0 1.2 copy-done
  123.2 0.7 copy-done.2
  123.9 20.8 %gather.1 = (f32[8,256,256]{2,1,0:T(8,128)S(1)}, f32[16,32,128]{2,1,0:T(8,128)S(1)}) custom-call(s32[8192]{0:T(1024)S(1)} %fusion.2.tile_ref, s32[8]{0:T(128)S(1)} %bitcast.44, bf16[32768,2,128]{2,1,0:T(2,128)(2,1)} %bitcast.45, bf16[8,1,2048]{2,1,0:T(2,128)(2,1)S(1)} %and_convert_fusion.live_ref, bf16[256,2048]{1,0:T(8,128)(2,1)S(1)} %copy.29.weight_ref, ...), custom_call_target="tpu_custom_call" | custom-call | flops 2415919104 | bytes 83886080 | tf_op jit(solution)/shard_map/gather/pallas_call | solution.py:72
  144.7 0.7 copy-done.1
  145.4 6.4 %all-to-all-start = ((f32[16,32,128]{2,1,0:T(8,128)}), f32[16,32,128]{2,1,0:T(8,128)S(1)}, u32[]{:S(2)}, u32[]{:S(2)}) async-start(f32[16,32,128]{2,1,0:T(8,128)} %copy-done.1), calls=%async_computation | async-start | bytes 524288 | tf_op jit(solution)/shard_map/all_to_all | solution.py:189
  151.8 0.9 fusion.21
  152.8 1.0 fusion.4
  153.9 6.3 %all-to-all-done = f32[16,32,128]{2,1,0:T(8,128)S(1)} async-done(((f32[16,32,128]{2,1,0:T(8,128)}), f32[16,32,128]{2,1,0:T(8,128)S(1)}, u32[]{:S(2)}, u32[]{:S(2)}) %all-to-all-start) | async-done | bytes 262176 | tf_op jit(solution)/shard_map/all_to_all | solution.py:189
  160.2 0.8 scan.1
  161.0 10.2 %all_to_all.10.below_ref = f32[16,32,128]{2,1,0:T(8,128)S(1)} all-to-all(f32[16,32,128]{2,1,0:T(8,128)S(1)} %bitcast.42), channel_id=1, replica_groups=mesh['front'=16,'tile'=32] {'front'}, dimensions={0} | all-to-all | bytes 524288 | tf_op jit(solution)/shard_map/all_to_all | solution.py:190
  171.3 2.5 %finish.1 = bf16[8,256,256]{2,1,0:T(8,128)(2,1)} custom-call(f32[8,256,256]{2,1,0:T(8,128)S(1)} %get-tuple-element.7.local_ref, f32[256,32]{1,0:T(8,128)S(1)} %copy.31.face_ref, f32[16,32,128]{2,1,0:T(8,128)S(1)} %all_to_all.10.below_ref), custom_call_target="tpu_custom_call" | custom-call | tf_op jit(solution)/shard_map/finish/pallas_call | solution.py:136
  (15 shorter events, 0.7 us)
Async XLA Ops:
  6.5 115.5 %all-gather.3.cloned.1.call-start = ((), (), s32[]{:S(2)}) async-start(), calls=%async_computation.2 | async-start | bytes 17301504 | tf_op jit(solution)/shard_map/all_gather | solution.py:172
  17.2 1.5 copy-start.3
  122.0 1.2 copy-start
  123.2 0.7 copy-start.2
  144.7 0.7 copy-start.1
  145.4 14.8 %all-to-all-start = ((f32[16,32,128]{2,1,0:T(8,128)}), f32[16,32,128]{2,1,0:T(8,128)S(1)}, u32[]{:S(2)}, u32[]{:S(2)}) async-start(f32[16,32,128]{2,1,0:T(8,128)} %copy-done.1), calls=%async_computation | async-start | bytes 524288 | tf_op jit(solution)/shard_map/all_to_all | solution.py:189
Sparse Core Ops, SparseCore 0:
  9.5 112.4 all-gather.2

commit v8 on v7

--- a/solution.py
+++ b/solution.py
@@ -15,7 +15,7 @@
 
 
 def gather_kernel(
-    tile_ref, count_ref, pool_hbm, live_ref, weight_ref, noise_ref, draw_ref,
+    tile_ref, count_ref, pool_hbm, live_ref, weight_ref, noise_ref, draw_ref, strip_ref,
     local_ref, edge_ref, pool, values, sems,
 ):
     blocks, cells, _ = local_ref.shape
@@ -63,19 +63,21 @@
     lax.fori_loop(0, blocks, block, 0)
 
 
-def gather_call(tile, count, pool, live, weight2, lower, draw, edge):
+def gather_call(tile, count, pool, live, weight2, lower, draw, strip):
     blocks, cells, realizations = draw.shape
     halves = realizations // LANES
+    edge = strip.shape[0]
     entries = tile.shape[0] // blocks
     smem = pl.BlockSpec(memory_space=pltpu.SMEM)
     vmem = pl.BlockSpec(memory_space=pltpu.VMEM)
+    hbm = pl.BlockSpec(memory_space=pl.ANY)
     return pl.pallas_call(
         gather_kernel,
         out_shape=(
             jax.ShapeDtypeStruct((blocks, cells, realizations), jnp.float32),
             jax.ShapeDtypeStruct((blocks * halves, edge, LANES), jnp.float32),
         ),
-        in_specs=[smem, smem, pl.BlockSpec(memory_space=pltpu.HBM), vmem, vmem, vmem, vmem],
+        in_specs=[smem, smem, pl.BlockSpec(memory_space=pltpu.HBM), vmem, vmem, vmem, vmem, hbm],
         out_specs=(vmem, vmem),
         scratch_shapes=[
             pltpu.VMEM(pool.shape, pool.dtype),
@@ -89,7 +91,7 @@
             transcendentals=0,
         ),
         name="gather",
-    )(tile, count, pool, live, weight2, lower, draw)
+    )(tile, count, pool, live, weight2, lower, draw, strip)
 
 
 def scan_kernel(strip_ref, face_ref, out_ref, near, far):
@@ -181,7 +183,7 @@
     weight2 = jnp.repeat(kriging_weight, 2, axis=1)
     strip = scan_strip(face_weight[-edge:], front_count)
     local, face = gather_call(
-        tile.reshape(-1), count, pieces, live, weight2, jnp.tril(noise_factor), normal_draw[0], edge
+        tile.reshape(-1), count, pieces, live, weight2, jnp.tril(noise_factor), normal_draw[0], strip
     )
     swap = functools.partial(
         lax.all_to_all, axis_name="front", split_axis=0, concat_axis=0, tiled=True

time: 182 us -> 181 us (level)
  blocking collectives: 10.2 us -> 24.2 us
  starting transfers between devices: 6.39 us -> 0.01 us
  waiting for transfers between devices: 108 us -> 103 us
  matrix products: 3.12 us -> 1.11 us
    all_to_all x0 -> x1, blocking collectives: none -> 14.1 us  [body(): below = scan_call(strip, swap(face).reshape(-1, LANES)).reshape(face.shape)]
    all_to_all x1 -> x0, starting transfers between devices: 6.39 us -> none  [body(): below = scan_call(strip, swap(face).reshape(-1, LANES)).reshape(face.shape)]
    all_to_all x1 -> x0, waiting for transfers between devices: 6.3 us -> none  [body(): below = scan_call(strip, swap(face).reshape(-1, LANES)).reshape(face.shape)]
    unnamed x10 -> x6, local copies, waits for them, and re-layouts: 4.69 us -> 4 us
  transfers between devices with their start and end apart: 2 -> 1, of which waited for: 2 -> 1; matrix products, arithmetic and copies ran while one was open for 9% -> 7% of each run, Pallas kernels for 0% -> 0%
where the time goes in v8:
time: 181 us; the launch traced here: 179 us
  waiting for transfers between devices  103 us (57%)
  Pallas kernels  24.2 us (13%)
  blocking collectives  24.2 us (13%)
  between operations  13.6 us (8%)
  local copies, waits for them, and re-layouts  9.26 us (5%)
  other arithmetic  4.18 us (2%)
    all_gather x1, waiting for transfers between devices, body(): gathered = lax.all_gather(pool[0], 'tile', tiled=True)  102 us
    pallas_call x1, Pallas kernels, gather_call(): pl.pallas_call(gather_kernel, out_shape=(jax.ShapeDtypeStruct((blocks, ce...  20.9 us
    all_to_all x1, blocking collectives, body(): below = scan_call(strip, swap(face).reshape(-1, LANES)).reshape(face.shape)  14.1 us
    all_to_all x1, blocking collectives, body(): return finish_call(local, face_weight, swap(below))[None]  10.1 us
    unnamed x6, local copies, waits for them, and re-layouts  4 us
  transfers between devices with their start and end apart: 1, of which 1 were waited for; matrix products, arithmetic and copies ran while one was open for 7% of the time, Pallas kernels for 0%

profile of v8, /device:TPU:1, one launch (start us, length us, event | category | flops | bytes accessed | tf_op | source)
XLA Modules:
  0.0 179.2 jit_solution(715338864922247650)
XLA Ops:
  6.5 0.7 all-gather.3.cloned.1.call-update
  7.3 0.9 copy.29.face_ref
  8.1 0.1 fusion.31
  8.3 0.2 fusion.17
  8.5 0.1 fusion.33
  8.6 0.2 fusion.21
  8.9 0.1 fusion.34
  9.0 0.3 fusion.4
  9.4 0.8 iota_compare_fusion
  10.2 0.5 and.48
  10.7 0.7 and.49
  11.3 1.2 copy.27
  12.5 0.8 fusion.12
  13.3 0.2 copy.24
  13.5 0.4 eq.37
  13.9 0.3 copy.25
  14.2 1.3 copy.28
  15.4 0.5 broadcast_in_dim.8
  16.0 0.4 reshape.109
  16.4 0.6 copy.30.weight_ref
  17.1 0.3 eq.40
  17.4 0.8 fusion.16
  18.2 0.8 fusion.2.tile_ref
  19.0 0.9 fusion.noise_ref
  20.1 102.0 %all-gather.3.cloned.1.call-done = bf16[1,32768,256]{2,1,0:T(8,128)(2,1)} async-done(((bf16[1,1024,256]{2,1,0:T(8,128)(2,1)}), bf16[1,32768,256]{2,1,0:T(8,128)(2,1)}) %all-gather.3.cloned.1.call-update) | async-done | bytes 16777232 | tf_op jit(solution)/shard_map/all_gather | solution.py:174
  122.0 1.2 copy-done
  123.2 0.7 copy-done.1
  123.9 20.9 %gather.1 = (f32[8,256,256]{2,1,0:T(8,128)S(1)}, f32[16,32,128]{2,1,0:T(8,128)S(1)}) custom-call(s32[8192]{0:T(1024)S(1)} %fusion.2.tile_ref, s32[8]{0:T(128)S(1)} %bitcast.44, bf16[32768,2,128]{2,1,0:T(2,128)(2,1)} %bitcast.45, bf16[8,1,2048]{2,1,0:T(2,128)(2,1)S(1)} %and_convert_fusion.live_ref, bf16[256,2048]{1,0:T(8,128)(2,1)S(1)} %copy.30.weight_ref, ...), custom_call_target="tpu_custom_call" | custom-call | flops 2415919104 | bytes 83886080 | tf_op jit(solution)/shard_map/gather/pallas_call | solution.py:74
  144.8 14.1 %all_to_all.10 = f32[16,32,128]{2,1,0:T(8,128)S(1)} all-to-all(f32[16,32,128]{2,1,0:T(8,128)S(1)} %get-tuple-element.8), channel_id=1, replica_groups=mesh['front'=16,'tile'=32] {'front'}, dimensions={0} | all-to-all | bytes 524288 | tf_op jit(solution)/shard_map/all_to_all | solution.py:191
  158.9 0.8 scan.1
  159.7 10.1 %all_to_all.11.below_ref = f32[16,32,128]{2,1,0:T(8,128)S(1)} all-to-all(f32[16,32,128]{2,1,0:T(8,128)S(1)} %bitcast.42), channel_id=1, replica_groups=mesh['front'=16,'tile'=32] {'front'}, dimensions={0} | all-to-all | bytes 524288 | tf_op jit(solution)/shard_map/all_to_all | solution.py:192
  169.8 2.5 %finish.1 = bf16[8,256,256]{2,1,0:T(8,128)(2,1)} custom-call(f32[8,256,256]{2,1,0:T(8,128)S(1)} %get-tuple-element.7.local_ref, f32[256,32]{1,0:T(8,128)S(1)} %copy.29.face_ref, f32[16,32,128]{2,1,0:T(8,128)S(1)} %all_to_all.11.below_ref), custom_call_target="tpu_custom_call" | custom-call | tf_op jit(solution)/shard_map/finish/pallas_call | solution.py:138
  (10 shorter events, 0.3 us)
Async XLA Ops:
  6.5 115.5 %all-gather.3.cloned.1.call-start = ((), (), s32[]{:S(2)}) async-start(), calls=%async_computation.2 | async-start | bytes 17301504 | tf_op jit(solution)/shard_map/all_gather | solution.py:174
  122.0 1.2 copy-start
  123.2 0.7 copy-start.1
Sparse Core Ops, SparseCore 0:
  9.5 112.4 all-gather.2
